TPU v7x, 128 devices: a whole 4x4x4 slice. The times are simulated.
128 devices in a mesh: img: 4 (over x), pix: 32 (over z, y, core).
Axes of the slice: x: 4, y: 4, z: 4, core: 2. Of those that a mesh axis runs over, the one named last changes fastest.
Arguments:
- step_ids: int32 [16], replicated, may hold values from 0 to 1023, as said below
- grid_table: float32 [1024, 12, 2048], P(('img', 'pix'))
- tile_image: int32 [2048], P(('img', 'pix')), may hold values from 0 to 3
- cell_index: int32 [2097152], P(('img', 'pix')), may hold values from 0 to 1910, as said below
- fractions: float32 [3, 2097152], P(None, ('img', 'pix')), may hold values from 0 to 1
- features: bfloat16 [64, 2097152], P(None, ('img', 'pix')), may hold values from -6 to 6
- head_weight: bfloat16 [3, 64], replicated, may hold values from -0.75 to 0.75
- head_bias: float32 [3], replicated, may hold values from -3 to 3
- cotangent: bfloat16 [3, 2097152], P(None, ('img', 'pix')), may hold values from -1.5 to 1.5
Outputs:
- owned_grads: float32 [256, 12, 2048], P(('img', 'pix'))
- head_grad: float32 [3, 64], replicated
- bias_grad: float32 [3], replicated
- feature_grad: bfloat16 [64, 2097152], P(None, ('img', 'pix'))
Inputs may be any that keep to these rules, and one draw needn't show every extreme that they name: `step_ids`: distinct; the holder step_ids // 8 has at most 2 of them, and some holder has exactly 2. `cell_index`: every corner cell stays inside the grid.
All inputs are finite; a program needn't handle non-finite values.
Results may differ from a plain program's by a relative error of at most 0.0049.
Values sent between devices are 32-bit elements; how exact they have to be, the bound alone decides.
A program may use at most 64 MiB of HBM per device.

v0:
```python
import jax
import jax.numpy as jnp
from jax import lax
from jax.sharding import PartitionSpec as P

GX = 16
GY = 16
GZ = 8
TILE = 1024
IMG_ROW = 4
OWN_MOST = 2


def tv_gradient(grids):
    shaped = grids.reshape(grids.shape[0], 12, GX, GY, GZ)
    summed = jnp.zeros_like(shaped)
    for axis in (2, 3, 4):
        diffs = jnp.diff(shaped, axis=axis)
        zero_shape = list(diffs.shape)
        zero_shape[axis] = 1
        zeros_rim = jnp.zeros(zero_shape, jnp.float32)
        summed = summed + (
            jnp.concatenate([zeros_rim, diffs], axis=axis)
            - jnp.concatenate([diffs, zeros_rim], axis=axis)
        )
    return (2.0 * 0.5 * summed).reshape(grids.shape)


def axis_weights(coord, frac, count):
    levels = jnp.arange(count, dtype=jnp.int32)[:, None]
    lower = jnp.where(levels == coord[None, :], 1.0 - frac[None, :], 0.0)
    upper = jnp.where(levels == coord[None, :] + 1, frac[None, :], 0.0)
    return lower + upper


def splat_matrix(cells, fracs):
    coord_x = cells // (GY * GZ)
    coord_y = cells // GZ % GY
    coord_z = cells % GZ
    along_x = axis_weights(coord_x, fracs[0], GX)
    along_y = axis_weights(coord_y, fracs[1], GY)
    along_z = axis_weights(coord_z, fracs[2], GZ)
    joined = along_x[:, None, None, :] * along_y[None, :, None, :] * along_z[None, None, :, :]
    return joined.reshape(GX * GY * GZ, cells.shape[0])


def shards(
    step_ids,
    grid_table,
    tile_image,
    cell_index,
    fractions,
    features,
    head_weight,
    head_bias,
    cotangent,
):
    tab_local = grid_table.shape[0]
    cell_count = grid_table.shape[2]
    img_step = step_ids.shape[0]
    pixel_count = cell_index.shape[0]
    tiles_here = pixel_count // TILE
    self_index = lax.axis_index(("img", "pix"))
    row_index = lax.axis_index("img")
    holders = step_ids // tab_local
    is_mine = holders == self_index
    contrib = jnp.where(is_mine[:, None, None], grid_table[step_ids % tab_local], 0.0)
    summed = lax.psum(contrib, ("img", "pix"))
    step_grids = lax.dynamic_slice_in_dim(summed, row_index * IMG_ROW, IMG_ROW, 0)
    logits = jnp.dot(head_weight, features, preferred_element_type=jnp.float32) + head_bias[:, None]
    colour = jax.nn.sigmoid(logits)
    upstream = cotangent.astype(jnp.float32)
    cells_tiled = cell_index.reshape(tiles_here, TILE)
    fracs_tiled = jnp.transpose(fractions.reshape(3, tiles_here, TILE), (1, 0, 2))
    upstream_tiled = jnp.transpose(upstream.reshape(3, tiles_here, TILE), (1, 0, 2))
    colour_tiled = jnp.transpose(colour.reshape(3, tiles_here, TILE), (1, 0, 2))
    image_range = jnp.arange(IMG_ROW, dtype=jnp.int32)

    def tile_step(grads_acc, tile_items):
        image_here, cells, fracs, upstream_tile, colour_tile = tile_items
        splat = splat_matrix(cells, fracs)
        grid_here = lax.dynamic_index_in_dim(step_grids, image_here, 0, keepdims=False)
        coeffs = jnp.dot(
            grid_here, splat, precision=lax.Precision.HIGHEST, preferred_element_type=jnp.float32
        )
        inputs = jnp.concatenate([colour_tile, jnp.ones((1, TILE), jnp.float32)], axis=0)
        d_coeffs = (upstream_tile[:, None, :] * inputs[None, :, :]).reshape(12, TILE)
        d_colour = (
            coeffs[0:3] * upstream_tile[0]
            + coeffs[4:7] * upstream_tile[1]
            + coeffs[8:11] * upstream_tile[2]
        )
        d_grid = lax.dot_general(
            d_coeffs,
            splat,
            (((1,), (1,)), ((), ())),
            precision=lax.Precision.HIGHEST,
            preferred_element_type=jnp.float32,
        )
        pick = (image_range == image_here).astype(jnp.float32)
        grads_acc = grads_acc + pick[:, None, None] * d_grid[None, :, :]
        return (grads_acc, d_colour)

    grads_init = jnp.zeros((IMG_ROW, 12, cell_count), jnp.float32)
    partial_value, d_colour_tiled = lax.scan(
        tile_step, grads_init, (tile_image, cells_tiled, fracs_tiled, upstream_tiled, colour_tiled)
    )
    d_colour = jnp.transpose(d_colour_tiled, (1, 0, 2)).reshape(3, pixel_count)
    d_logits = d_colour * colour * (1.0 - colour)
    d_half = d_logits.astype(jnp.bfloat16)
    feature_grad = lax.dot_general(
        head_weight, d_half, (((0,), (0,)), ((), ())), preferred_element_type=jnp.float32
    ).astype(jnp.bfloat16)
    head_part = lax.dot_general(
        d_half, features, (((1,), (1,)), ((), ())), preferred_element_type=jnp.float32
    )
    bias_part = jnp.sum(d_logits, axis=1)
    head_grad, bias_grad = lax.psum((head_part, bias_part), ("img", "pix"))
    placed = jnp.zeros((img_step, 12, cell_count), jnp.float32)
    placed = lax.dynamic_update_slice_in_dim(placed, partial_value, row_index * IMG_ROW, 0)
    step_grads = lax.psum(placed, ("img", "pix"))
    positions = jnp.arange(img_step, dtype=jnp.int32)
    earlier = (positions[None, :] < positions[:, None]) & is_mine[None, :]
    order_rank = jnp.sum(earlier.astype(jnp.int32), axis=1)
    slot_range = jnp.arange(OWN_MOST, dtype=jnp.int32)
    selector = ((order_rank[None, :] == slot_range[:, None]) & is_mine[None, :]).astype(jnp.float32)
    owned_data = jnp.einsum("st,tkc->skc", selector, step_grads, precision=lax.Precision.HIGHEST)
    owned_grids = jnp.einsum("st,tkc->skc", selector, contrib, precision=lax.Precision.HIGHEST)
    owned_grads = owned_data + tv_gradient(owned_grids)
    return (owned_grads, head_grad, bias_grad, feature_grad)


def solution(mesh):
    return jax.shard_map(
        shards,
        mesh=mesh,
        in_specs=(
            P(),
            P(("img", "pix"), None, None),
            P(("img", "pix")),
            P(("img", "pix")),
            P(None, ("img", "pix")),
            P(None, ("img", "pix")),
            P(),
            P(),
            P(None, ("img", "pix")),
        ),
        out_specs=(P(("img", "pix"), None, None), P(), P(), P(None, ("img", "pix"))),
        check_vma=False,
    )
```

profile of v0, /device:TPU:1, one launch (start us, length us, event | category | flops | bytes accessed | tf_op | source)
XLA Modules:
  0.0 751.0 jit_solution(3122320382121305810)
XLA Ops:
  8.7 4.5 gather_fusion
  13.2 2.8 broadcast_select_fusion
  16.2 2.2 fusion.17
  18.3 3.4 reshape.396
  21.7 4.7 slice_subtract_fusion.2
  28.1 5.6 slice_subtract_fusion
  33.7 2.3 slice_subtract_fusion.1
  36.0 132.3 %all-reduce.11.cloned.1.call-done = f32[16,12,2048]{2,0,1:T(8,128)} async-done(((f32[16,12,2048]{2,0,1:T(8,128)}), f32[16,12,2048]{2,0,1:T(8,128)}) %all-reduce.11.cloned.1.call-update) | async-done | bytes 1572880 | tf_op jit(solution)/shard_map/psum | solution.py:68
  168.3 2.0 constant_dynamic-slice_fusion.8
  170.3 421.3 %while.16 = (s32[]{:T(128)}, f32[4,12,2048]{2,1,0:T(8,128)S(1)}, f32[16,3,1024]{2,1,0:T(4,128)S(1)}, s32[16]{0:T(128)S(1)}, f32[16,3,1024]{2,1,0:T(4,128)}, /*in...) while((s32[]{:T(128)}, f32[4,12,2048]{2,1,0:T(8,128)S(1)}, ...), condition=%wide.region_3.4_spmd.clone, body=%wide.region_2.3_spmd.clone.sunk | while | flops 606914560 | bytes 29458716 | solution.py:105
  171.5 4.3 broadcast_multiply_fusion.8
  176.5 9.2 %fusion.44 = f32[12,2048]{1,0:T(8,128)S(1)} fusion(f32[12,1024]{1,0:T(8,128)S(1)} %mul.310, f32[2048,1024]{1,0:T(8,128)} %bitcast.99), kind=kOutput, calls=%fused_computation.94.clone.1 | convolution fusion | flops 301989888 | bytes 8536064 | tf_op jit(solution)/shard_map/while/body/eval_jaxpr/dot_general | solution.py:93
  190.2 6.4 fusion.45
  197.8 4.3 broadcast_multiply_fusion.8
  202.9 9.2 %fusion.44 = f32[12,2048]{1,0:T(8,128)S(1)} fusion(f32[12,1024]{1,0:T(8,128)S(1)} %mul.310, f32[2048,1024]{1,0:T(8,128)} %bitcast.99), kind=kOutput, calls=%fused_computation.94.clone.1 | convolution fusion | flops 301989888 | bytes 8536064 | tf_op jit(solution)/shard_map/while/body/eval_jaxpr/dot_general | solution.py:93
  216.5 6.4 fusion.45
  224.1 4.3 broadcast_multiply_fusion.8
  229.2 9.2 %fusion.44 = f32[12,2048]{1,0:T(8,128)S(1)} fusion(f32[12,1024]{1,0:T(8,128)S(1)} %mul.310, f32[2048,1024]{1,0:T(8,128)} %bitcast.99), kind=kOutput, calls=%fused_computation.94.clone.1 | convolution fusion | flops 301989888 | bytes 8536064 | tf_op jit(solution)/shard_map/while/body/eval_jaxpr/dot_general | solution.py:93
  242.8 6.4 fusion.45
  250.5 4.3 broadcast_multiply_fusion.8
  255.5 9.2 %fusion.44 = f32[12,2048]{1,0:T(8,128)S(1)} fusion(f32[12,1024]{1,0:T(8,128)S(1)} %mul.310, f32[2048,1024]{1,0:T(8,128)} %bitcast.99), kind=kOutput, calls=%fused_computation.94.clone.1 | convolution fusion | flops 301989888 | bytes 8536064 | tf_op jit(solution)/shard_map/while/body/eval_jaxpr/dot_general | solution.py:93
  269.1 6.4 fusion.45
  276.8 4.3 broadcast_multiply_fusion.8
  281.9 9.2 %fusion.44 = f32[12,2048]{1,0:T(8,128)S(1)} fusion(f32[12,1024]{1,0:T(8,128)S(1)} %mul.310, f32[2048,1024]{1,0:T(8,128)} %bitcast.99), kind=kOutput, calls=%fused_computation.94.clone.1 | convolution fusion | flops 301989888 | bytes 8536064 | tf_op jit(solution)/shard_map/while/body/eval_jaxpr/dot_general | solution.py:93
  295.5 6.4 fusion.45
  303.1 4.3 broadcast_multiply_fusion.8
  308.2 9.2 %fusion.44 = f32[12,2048]{1,0:T(8,128)S(1)} fusion(f32[12,1024]{1,0:T(8,128)S(1)} %mul.310, f32[2048,1024]{1,0:T(8,128)} %bitcast.99), kind=kOutput, calls=%fused_computation.94.clone.1 | convolution fusion | flops 301989888 | bytes 8536064 | tf_op jit(solution)/shard_map/while/body/eval_jaxpr/dot_general | solution.py:93
  321.8 6.4 fusion.45
  329.5 4.3 broadcast_multiply_fusion.8
  334.6 9.2 %fusion.44 = f32[12,2048]{1,0:T(8,128)S(1)} fusion(f32[12,1024]{1,0:T(8,128)S(1)} %mul.310, f32[2048,1024]{1,0:T(8,128)} %bitcast.99), kind=kOutput, calls=%fused_computation.94.clone.1 | convolution fusion | flops 301989888 | bytes 8536064 | tf_op jit(solution)/shard_map/while/body/eval_jaxpr/dot_general | solution.py:93
  348.2 6.4 fusion.45
  355.8 4.3 broadcast_multiply_fusion.8
  360.9 9.2 %fusion.44 = f32[12,2048]{1,0:T(8,128)S(1)} fusion(f32[12,1024]{1,0:T(8,128)S(1)} %mul.310, f32[2048,1024]{1,0:T(8,128)} %bitcast.99), kind=kOutput, calls=%fused_computation.94.clone.1 | convolution fusion | flops 301989888 | bytes 8536064 | tf_op jit(solution)/shard_map/while/body/eval_jaxpr/dot_general | solution.py:93
  374.5 6.4 fusion.45
  382.1 4.3 broadcast_multiply_fusion.8
  387.2 9.2 %fusion.44 = f32[12,2048]{1,0:T(8,128)S(1)} fusion(f32[12,1024]{1,0:T(8,128)S(1)} %mul.310, f32[2048,1024]{1,0:T(8,128)} %bitcast.99), kind=kOutput, calls=%fused_computation.94.clone.1 | convolution fusion | flops 301989888 | bytes 8536064 | tf_op jit(solution)/shard_map/while/body/eval_jaxpr/dot_general | solution.py:93
  400.8 6.4 fusion.45
  408.5 4.3 broadcast_multiply_fusion.8
  413.5 9.2 %fusion.44 = f32[12,2048]{1,0:T(8,128)S(1)} fusion(f32[12,1024]{1,0:T(8,128)S(1)} %mul.310, f32[2048,1024]{1,0:T(8,128)} %bitcast.99), kind=kOutput, calls=%fused_computation.94.clone.1 | convolution fusion | flops 301989888 | bytes 8536064 | tf_op jit(solution)/shard_map/while/body/eval_jaxpr/dot_general | solution.py:93
  427.1 6.4 fusion.45
  434.8 4.3 broadcast_multiply_fusion.8
  439.9 9.2 %fusion.44 = f32[12,2048]{1,0:T(8,128)S(1)} fusion(f32[12,1024]{1,0:T(8,128)S(1)} %mul.310, f32[2048,1024]{1,0:T(8,128)} %bitcast.99), kind=kOutput, calls=%fused_computation.94.clone.1 | convolution fusion | flops 301989888 | bytes 8536064 | tf_op jit(solution)/shard_map/while/body/eval_jaxpr/dot_general | solution.py:93
  453.5 6.4 fusion.45
  461.1 4.3 broadcast_multiply_fusion.8
  466.2 9.2 %fusion.44 = f32[12,2048]{1,0:T(8,128)S(1)} fusion(f32[12,1024]{1,0:T(8,128)S(1)} %mul.310, f32[2048,1024]{1,0:T(8,128)} %bitcast.99), kind=kOutput, calls=%fused_computation.94.clone.1 | convolution fusion | flops 301989888 | bytes 8536064 | tf_op jit(solution)/shard_map/while/body/eval_jaxpr/dot_general | solution.py:93
  479.8 6.4 fusion.45
  487.5 4.3 broadcast_multiply_fusion.8
  492.5 9.2 %fusion.44 = f32[12,2048]{1,0:T(8,128)S(1)} fusion(f32[12,1024]{1,0:T(8,128)S(1)} %mul.310, f32[2048,1024]{1,0:T(8,128)} %bitcast.99), kind=kOutput, calls=%fused_computation.94.clone.1 | convolution fusion | flops 301989888 | bytes 8536064 | tf_op jit(solution)/shard_map/while/body/eval_jaxpr/dot_general | solution.py:93
  506.1 6.4 fusion.45
  513.8 4.3 broadcast_multiply_fusion.8
  518.9 9.2 %fusion.44 = f32[12,2048]{1,0:T(8,128)S(1)} fusion(f32[12,1024]{1,0:T(8,128)S(1)} %mul.310, f32[2048,1024]{1,0:T(8,128)} %bitcast.99), kind=kOutput, calls=%fused_computation.94.clone.1 | convolution fusion | flops 301989888 | bytes 8536064 | tf_op jit(solution)/shard_map/while/body/eval_jaxpr/dot_general | solution.py:93
  532.5 6.4 fusion.45
  540.1 4.3 broadcast_multiply_fusion.8
  545.2 9.2 %fusion.44 = f32[12,2048]{1,0:T(8,128)S(1)} fusion(f32[12,1024]{1,0:T(8,128)S(1)} %mul.310, f32[2048,1024]{1,0:T(8,128)} %bitcast.99), kind=kOutput, calls=%fused_computation.94.clone.1 | convolution fusion | flops 301989888 | bytes 8536064 | tf_op jit(solution)/shard_map/while/body/eval_jaxpr/dot_general | solution.py:93
  558.8 6.4 fusion.45
  566.5 4.3 broadcast_multiply_fusion.8
  571.5 9.2 %fusion.44 = f32[12,2048]{1,0:T(8,128)S(1)} fusion(f32[12,1024]{1,0:T(8,128)S(1)} %mul.310, f32[2048,1024]{1,0:T(8,128)} %bitcast.99), kind=kOutput, calls=%fused_computation.94.clone.1 | convolution fusion | flops 301989888 | bytes 8536064 | tf_op jit(solution)/shard_map/while/body/eval_jaxpr/dot_general | solution.py:93
  585.2 6.4 fusion.45
  594.0 9.6 %subtract_add_fusion = f32[2,12,16,16,8]{4,3,2,0,1:T(8,128)} fusion(f32[2,12,16,16,7]{4,3,2,0,1:T(8,128)} %slice_subtract_fusion, f32[2,12,16,15,8]{4,3,2,0,1:T(8,128)} %slice_subtract_fusion.1, f32[2,12,15,16,8]{4,3,2,0,1:T(8,128)} %slice_subtract_fusion.2), kind=kLoop, calls=%fused_computation.63 | loop fusion | flops 245760 | bytes 737280 | tf_op jit(solution)/shard_map/add | solution.py:22
  603.5 3.3 reshape.397
  607.7 63.8 %all-reduce.7 = (f32[3,64]{1,0:T(4,128)}, f32[3]{0:T(128)}) all-reduce(f32[3,64]{1,0:T(4,128)S(1)} %fusion.14, f32[3]{0:T(128)S(1)} %fusion.25), channel_id=1, replica_groups=mesh['img'=4,'pix'=32] {'img','pix'}, use_global_device_ids=true, to_apply=%region_5.6 | all-reduce | flops 195 | bytes 1560 | tf_op jit(solution)/shard_map/psum | solution.py:118
  671.5 2.1 fusion.8
  673.6 67.8 %all-reduce.13.cloned.1.call-done = f32[16,12,2048]{2,0,1:T(8,128)} async-done(((f32[16,12,2048]{2,0,1:T(8,128)}), f32[16,12,2048]{2,0,1:T(8,128)}) %all-reduce.13.cloned.1.call-update) | async-done | bytes 1572880 | tf_op jit(solution)/shard_map/psum | solution.py:121
  741.4 2.7 convolution_add_fusion.1
  (335 shorter events, 76.8 us)
Async XLA Ops:
  7.2 19.3 %copy-start = (bf16[64,16384]{1,0:T(8,128)(2,1)S(1)}, bf16[64,16384]{1,0:T(8,128)(2,1)}, u32[]{:S(2)}) copy-start(bf16[64,16384]{1,0:T(8,128)(2,1)} %param.16) | copy-start | bytes 6291460
  7.2 161.1 %all-reduce.11.cloned.1.call-start = ((), (), s32[]{:S(2)}) async-start(), calls=%async_computation | async-start | bytes 3145728 | tf_op jit(solution)/shard_map/psum | solution.py:68
  16.0 725.4 %all-reduce.13.cloned.1.call-start = ((), (), s32[]{:S(2)}) async-start(), calls=%async_computation.1 | async-start | bytes 3145728 | tf_op jit(solution)/shard_map/psum | solution.py:121
  21.7 4.7 copy-start.4
  21.7 4.7 copy-start.5
  26.4 0.9 copy-start.2
  26.5 1.6 copy-start.3
  28.1 5.6 copy-start.1
  33.7 136.5 %copy-start.6 = (s32[16]{0:T(128)S(1)}, s32[16]{0:T(128)}, u32[]{:S(2)}) copy-start(s32[16]{0:T(128)} %param.13) | copy-start | bytes 196
Sparse Core Ops, SparseCore 0:
  16.1 152.1 all-reduce.10
  594.1 147.2 all-reduce.12
where the time goes:
time: 755 us; the launch traced here: 751 us
  matrix products  257 us (34%)
  waiting for transfers between devices  200 us (26%)
  other arithmetic  113 us (15%)
  local copies, waits for them, and re-layouts  69.4 us (9%)
  blocking collectives  63.8 us (8%)
  loops' own time  33.1 us (4%)
  between operations  14.1 us (2%)
    dot_general x16, matrix products, tile_step(): lax.dot_general(d_coeffs, splat, (((1,), (1,)), ((), ())), precision=lax....  147 us
    psum x1, waiting for transfers between devices, shards(): summed = lax.psum(contrib, ('img', 'pix'))  132 us
    dot_general x16, matrix products, tile_step(): jnp.dot(grid_here, splat, precision=lax.Precision.HIGHEST, preferred_elem...  102 us
    mul x32, other arithmetic, splat_matrix(): along_x[:, None, None, :] * along_y[None, :, None, :]  70.4 us
    psum x1, waiting for transfers between devices, shards(): step_grads = lax.psum(placed, ('img', 'pix'))  67.8 us
    psum x1, blocking collectives, shards(): head_grad, bias_grad = lax.psum((head_part, bias_part), ('img', 'pix'))  63.8 us
    another operation x1, loops' own time, shards(): lax.scan(tile_step, grads_init, (tile_image, cells_tiled, fracs_tiled, up...  33.1 us
    dynamic_slice x16, local copies, waits for them, and re-layouts, tile_step(): lax.dynamic_index_in_dim(step_grids, image_here, 0, keepdims=False)  17.6 us
  transfers between devices with their start and end apart: 2, of which 2 were waited for; matrix products, arithmetic and copies ran while one was open for 5% of the time, Pallas kernels for 0%

commit v1 on v0

v1 whole, which is shorter than its diff:
```python
import functools

import jax
import jax.numpy as jnp
from jax import lax
from jax.experimental import pallas as pl
from jax.experimental.pallas import tpu as pltpu
from jax.sharding import PartitionSpec as P

GX = 16
GY = 16
GZ = 8
YZ = GY * GZ
CELLS = GX * YZ
COEF = 12
TILE = 1024
IMG_ROW = 4
OWN_MOST = 2
ROWS = COEF * GX
USED = 9 * GX
MESH = pl.DeviceIdType.MESH
NT = (((1,), (1,)), ((), ()))


def spread(block):
    return jnp.concatenate(
        [jnp.broadcast_to(block[s : s + 1, :], (8, 128)) for s in range(8)], axis=1
    )


def hat(coord, level, low, high):
    return jnp.where(coord == level, low, jnp.where(coord == level - 1, high, 0.0))


def kernel(
    planes,
    rows_x,
    ids_ref,
    tile_ref,
    bias_ref,
    table_ref,
    cell_ref,
    frac_ref,
    feat_ref,
    weight_ref,
    cot_ref,
    owned_ref,
    head_ref,
    fgrad_ref,
    splat_ref,
    uax_ref,
    colour_ref,
    acc_ref,
    sib_ref,
    total_ref,
    grid_f32,
    grid_ref,
    tv_ref,
    stat_ref,
    head_acc,
    bias_acc,
    holder_q,
    holder_g,
    rank_ref,
    dest_ref,
    g1_send,
    g1_recv,
    g2_send,
    g2_recv,
    g3_send,
    g3_recv,
    r1_send,
    r1_recv,
    r2_send,
    r2_recv,
    r3_send,
    r3_recv,
    h1_recv,
    h2_send,
    h2_recv,
    sib_sems,
    plane_ss,
    plane_rs,
    line_ss,
    line_rs,
):
    tiles = cell_ref.shape[0] // 8
    images = ids_ref.shape[0]
    groups = rows_x * 2
    my_x = lax.axis_index("img")
    my_pix = lax.axis_index("pix")
    my_q = my_pix // 2
    my_c = my_pix % 2
    my_g = my_x * 2 + my_c
    my_dev = my_x * (planes * 2) + my_pix

    def plane_copy(stage, q, src, dst):
        return pltpu.make_async_remote_copy(
            src_ref=src,
            dst_ref=dst,
            send_sem=plane_ss.at[stage, q],
            recv_sem=plane_rs.at[stage, my_q],
            device_id={"img": my_x, "pix": q * 2 + my_c},
            device_id_type=MESH,
        )

    def line_copy(stage, g, src, dst):
        return pltpu.make_async_remote_copy(
            src_ref=src,
            dst_ref=dst,
            send_sem=line_ss.at[stage, g],
            recv_sem=line_rs.at[stage, my_g],
            device_id={"img": g // 2, "pix": my_q * 2 + g % 2},
            device_id_type=MESH,
        )

    def plane_each(fn):
        def step(o, carry):
            fn((my_q + o) % planes)
            return carry

        lax.fori_loop(1, planes, step, 0)

    def line_each(fn):
        def step(o, carry):
            fn((my_g + o) % groups)
            return carry

        lax.fori_loop(1, groups, step, 0)

    def plane_arrive(stage, buf):
        def one(q):
            pltpu.make_async_remote_copy(
                src_ref=buf.at[q],
                dst_ref=buf.at[q],
                send_sem=plane_ss.at[stage, q],
                recv_sem=plane_rs.at[stage, q],
                device_id={"img": my_x, "pix": q * 2 + my_c},
                device_id_type=MESH,
            ).wait_recv()

        plane_each(one)

    def line_arrive(stage, buf):
        def one(g):
            pltpu.make_async_remote_copy(
                src_ref=buf.at[g],
                dst_ref=buf.at[g],
                send_sem=line_ss.at[stage, g],
                recv_sem=line_rs.at[stage, g],
                device_id={"img": g // 2, "pix": my_q * 2 + g % 2},
                device_id_type=MESH,
            ).wait_recv()

        line_each(one)

    barrier = pltpu.get_barrier_semaphore()

    def greet_plane(q):
        pl.semaphore_signal(
            barrier,
            inc=1,
            device_id={"img": my_x, "pix": q * 2 + my_c},
            device_id_type=MESH,
        )

    def greet_line(g):
        pl.semaphore_signal(
            barrier,
            inc=1,
            device_id={"img": g // 2, "pix": my_q * 2 + g % 2},
            device_id_type=MESH,
        )

    plane_each(greet_plane)
    line_each(greet_line)

    holders = []
    ranks = []
    for i in range(images):
        holder = ids_ref[i] // table_ref.shape[0]
        rank = jnp.int32(0)
        for other in holders:
            rank = rank + jnp.where(other == holder, 1, 0)
        holders.append(holder)
        ranks.append(rank)
        hx = holder // (planes * 2)
        hp = holder % (planes * 2)
        holder_q[i] = hp // 2
        holder_g[i] = hx * 2 + hp % 2
        rank_ref[i] = jnp.minimum(rank, OWN_MOST - 1)

    own_row = [jnp.int32(0)] * OWN_MOST
    own_has = [jnp.int32(0)] * OWN_MOST
    for i in range(images):
        for s in range(OWN_MOST):
            hit = (holders[i] == my_dev) & (ranks[i] == s)
            own_row[s] = jnp.where(hit, ids_ref[i] % table_ref.shape[0], own_row[s])
            own_has[s] = jnp.where(hit, 1, own_has[s])

    for s in range(OWN_MOST):
        for q in range(planes):
            g1_send[q, s] = table_ref[own_row[s], :, q * YZ : (q + 1) * YZ]

    pl.semaphore_wait(barrier, planes - 1 + groups - 1)
    plane_each(lambda q: plane_copy(0, q, g1_send.at[q], g1_recv.at[my_q]).start())
    g1_recv[my_q] = g1_send[my_q]

    def find_dest(q, carry):
        dev = my_x * (planes * 2) + q * 2 + my_c
        for s in range(OWN_MOST):
            found = jnp.int32(images)
            for i in range(images):
                found = jnp.where((holders[i] == dev) & (ranks[i] == s), i, found)
            dest_ref[q * OWN_MOST + s] = found
        return carry

    lax.fori_loop(0, planes, find_dest, 0)

    lane = lax.broadcasted_iota(jnp.int32, (COEF, YZ), 1)
    for s in range(OWN_MOST):
        for q in range(planes):
            here = g1_send[q, s]
            total = jnp.zeros((COEF, YZ), jnp.float32)
            if q > 0:
                total = total + (here - g1_send[q - 1, s])
            if q < planes - 1:
                total = total - (g1_send[q + 1, s] - here)
            for step, first, last in (
                (GZ, lane >= GZ, lane < YZ - GZ),
                (1, lane % GZ != 0, lane % GZ != GZ - 1),
            ):
                before = jnp.where(first, here - pltpu.roll(here, step, 1), 0.0)
                after = jnp.where(last, pltpu.roll(here, YZ - step, 1) - here, 0.0)
                total = total + (before - after)
            tv_ref[s, :, q * YZ : (q + 1) * YZ] = jnp.where(own_has[s] == 1, total, 0.0)

    acc_ref[...] = jnp.zeros_like(acc_ref)
    head_acc[...] = jnp.zeros_like(head_acc)
    bias_acc[...] = jnp.zeros_like(bias_acc)

    def gather_two():
        plane_arrive(0, g1_recv)
        for i in range(images):
            g2_send[i // IMG_ROW, i % IMG_ROW] = g1_recv[holder_q[i], rank_ref[i]]
        line_each(
            lambda g: line_copy(0, g, g2_send.at[g // 2], g2_recv.at[my_g]).start()
        )
        g2_recv[my_g] = g2_send[my_x]

    def gather_three():
        line_arrive(0, g2_recv)
        for i in range(IMG_ROW):
            g3_send[i] = g2_recv[holder_g[my_x * IMG_ROW + i], i]
        plane_each(lambda q: plane_copy(1, q, g3_send, g3_recv.at[my_q]).start())
        g3_recv[my_q] = g3_send[...]

    def splat_tile(t, carry):
        @pl.when(t == tiles // 4)
        def _():
            gather_two()

        @pl.when(t == tiles // 2)
        def _():
            gather_three()

        px = pl.ds(pl.multiple_of(t * TILE, TILE), TILE)
        cell = spread(cell_ref[pl.ds(pl.multiple_of(t * 8, 8), 8), :])
        cx = cell // YZ
        cy = (cell // GZ) % GY
        cz = cell % GZ
        fx = jnp.broadcast_to(frac_ref[0:1, px], (8, TILE))
        fy = jnp.broadcast_to(frac_ref[1:2, px], (8, TILE))
        fz = jnp.broadcast_to(frac_ref[2:3, px], (8, TILE))
        low_level = lax.broadcasted_iota(jnp.int32, (8, TILE), 0)
        az = hat(cz, low_level, 1.0 - fz, fz)
        gy = 1.0 - fy
        for y in range(0, GY, 2):
            pair = jnp.concatenate(
                [hat(cy, y, gy, fy) * az, hat(cy, y + 1, gy, fy) * az], axis=0
            )
            big = pair.astype(jnp.bfloat16)
            rest = (pair - big.astype(jnp.float32)).astype(jnp.bfloat16)
            splat_ref[t, y * GZ : (y + 2) * GZ, :] = big
            splat_ref[t, YZ + y * GZ : YZ + (y + 2) * GZ, :] = rest
        gx = 1.0 - fx
        ax = jnp.concatenate(
            [hat(cx, low_level, gx, fx), hat(cx, low_level + 8, gx, fx)], axis=0
        )
        logits = jnp.dot(
            weight_ref[...], feat_ref[:, px], preferred_element_type=jnp.float32
        )
        chan = lax.broadcasted_iota(jnp.int32, (3, TILE), 0)
        bias = jnp.where(
            chan == 0, bias_ref[0], jnp.where(chan == 1, bias_ref[1], bias_ref[2])
        )
        colour = 1.0 / (1.0 + jnp.exp(-(logits + bias)))
        colour_ref[t, 0:3, :] = colour
        parts = []
        for k in range(3):
            u = jnp.broadcast_to(cot_ref[k : k + 1, px].astype(jnp.float32), (GX, TILE))
            uax = u * ax
            uax_ref[t, k * GX : (k + 1) * GX, :] = uax
            for j in range(3):
                col = jnp.broadcast_to(colour[j : j + 1, :], (GX, TILE))
                parts.append((uax * col).astype(jnp.bfloat16))
            parts.append(uax.astype(jnp.bfloat16))
        left = jnp.concatenate(parts, axis=0)
        both = lax.dot_general(
            left, splat_ref[t], NT, preferred_element_type=jnp.float32
        )
        grads = both[:, :YZ] + both[:, YZ:]
        image = tile_ref[t]
        for i in range(IMG_ROW):
            acc_ref[i] += jnp.where(image == i, grads, 0.0)
        return carry

    lax.fori_loop(0, tiles, splat_tile, 0)

    sibling = pltpu.make_async_remote_copy(
        src_ref=acc_ref.at[pl.ds(2 * (1 - my_c), 2)],
        dst_ref=sib_ref,
        send_sem=sib_sems.at[0],
        recv_sem=sib_sems.at[1],
        device_id={"img": my_x, "pix": my_q * 2 + 1 - my_c},
        device_id_type=MESH,
    )
    sibling.start()

    plane_arrive(1, g3_recv)
    for i in range(IMG_ROW):
        for q in range(planes):
            grid_f32[i, pl.ds(q, COEF, stride=GX), :] = g3_recv[q, i]
    for i in range(IMG_ROW):
        full = jnp.concatenate(
            [grid_f32[i, 4 * k * GX : (4 * k + 3) * GX, :] for k in range(3)], axis=0
        )
        big = full.astype(jnp.bfloat16)
        rest = (full - big.astype(jnp.float32)).astype(jnp.bfloat16)
        grid_ref[i, 0:USED, 0:YZ] = big
        grid_ref[i, 0:USED, YZ : 2 * YZ] = big
        grid_ref[i, USED : 2 * USED, 0:YZ] = rest
        grid_ref[i, USED : 2 * USED, YZ : 2 * YZ] = rest

    sibling.wait()
    for i in range(2):
        total_ref[i] = acc_ref[2 * my_c + i] + sib_ref[i]
    for q in range(planes):
        for i in range(2):
            r1_send[q, i] = total_ref[i, pl.ds(q, COEF, stride=GX), :]
    plane_each(lambda q: plane_copy(2, q, r1_send.at[q], r1_recv.at[my_q]).start())
    r1_recv[my_q] = r1_send[my_q]

    def reduce_two():
        plane_arrive(2, r1_recv)
        for i in range(2):
            total = r1_recv[0, i]
            for q in range(1, planes):
                total = total + r1_recv[q, i]
            r2_send[i] = total
        line_each(lambda g: line_copy(1, g, r2_send, r2_recv.at[my_g]).start())
        r2_recv[my_g] = r2_send[...]
        r2_recv[groups] = jnp.zeros_like(r2_send)

    def reduce_three():
        line_arrive(1, r2_recv)
        for q in range(planes):
            for s in range(OWN_MOST):
                i = dest_ref[q * OWN_MOST + s]
                r3_send[q, s] = r2_recv[i // 2, i % 2]
        plane_each(lambda q: plane_copy(3, q, r3_send.at[q], r3_recv.at[my_q]).start())
        r3_recv[my_q] = r3_send[my_q]

    weight_t = weight_ref[...].astype(jnp.float32).T.astype(jnp.bfloat16)

    def slice_tile(t, carry):
        @pl.when(t == tiles // 2)
        def _():
            reduce_two()

        @pl.when(t == tiles - tiles // 4)
        def _():
            reduce_three()

        px = pl.ds(pl.multiple_of(t * TILE, TILE), TILE)
        wide = jnp.dot(
            grid_ref[tile_ref[t]], splat_ref[t], preferred_element_type=jnp.float32
        )
        sums = []
        for j in range(3):
            total = None
            for k in range(3):
                at = (3 * k + j) * GX
                coef = wide[at : at + GX] + wide[USED + at : USED + at + GX]
                term = coef * uax_ref[t, k * GX : (k + 1) * GX, :]
                total = term if total is None else total + term
            sums.append(jnp.sum(total, axis=0, keepdims=True))
        d_colour = jnp.concatenate(sums, axis=0)
        colour = colour_ref[t, 0:3, :]
        d_logits = d_colour * colour * (1.0 - colour)
        d_half = d_logits.astype(jnp.bfloat16)
        fgrad_ref[:, px] = jnp.dot(
            weight_t, d_half, preferred_element_type=jnp.float32
        ).astype(jnp.bfloat16)
        head_acc[...] += lax.dot_general(
            d_half, feat_ref[:, px], NT, preferred_element_type=jnp.float32
        )
        bias_acc[...] += d_logits
        return carry

    lax.fori_loop(0, tiles, slice_tile, 0)

    bias_sum = jnp.sum(bias_acc[...], axis=1, keepdims=True)
    stat_ref[...] = jnp.zeros_like(stat_ref)
    stat_ref[0:3, :] = jnp.concatenate(
        [head_acc[...], jnp.broadcast_to(bias_sum, head_acc.shape)], axis=1
    )
    plane_each(lambda q: plane_copy(4, q, stat_ref, h1_recv.at[my_q]).start())
    h1_recv[my_q] = stat_ref[...]
    plane_arrive(3, r3_recv)
    for s in range(OWN_MOST):
        for q in range(planes):
            cols = slice(q * YZ, (q + 1) * YZ)
            owned_ref[s, :, cols] = r3_recv[q, s] + tv_ref[s, :, cols]
    plane_arrive(4, h1_recv)
    total = h1_recv[0]
    for q in range(1, planes):
        total = total + h1_recv[q]
    h2_send[...] = total
    line_each(lambda g: line_copy(2, g, h2_send, h2_recv.at[my_g]).start())
    h2_recv[my_g] = total
    line_arrive(2, h2_recv)
    total = h2_recv[0]
    for g in range(1, groups):
        total = total + h2_recv[g]
    head_ref[...] = total

    def plane_sent(q):
        plane_copy(0, q, g1_send.at[q], g1_recv.at[my_q]).wait_send()
        plane_copy(1, q, g3_send, g3_recv.at[my_q]).wait_send()
        plane_copy(2, q, r1_send.at[q], r1_recv.at[my_q]).wait_send()
        plane_copy(3, q, r3_send.at[q], r3_recv.at[my_q]).wait_send()
        plane_copy(4, q, stat_ref, h1_recv.at[my_q]).wait_send()

    def line_sent(g):
        line_copy(0, g, g2_send.at[g // 2], g2_recv.at[my_g]).wait_send()
        line_copy(1, g, r2_send, r2_recv.at[my_g]).wait_send()
        line_copy(2, g, h2_send, h2_recv.at[my_g]).wait_send()

    plane_each(plane_sent)
    line_each(line_sent)


def shards(planes, rows_x, ids, table, tile_image, cell, frac, feat, weight, bias, cot):
    pixels = cell.shape[0]
    tiles = pixels // TILE
    groups = rows_x * 2
    images = ids.shape[0]
    f32, bf16 = jnp.float32, jnp.bfloat16
    chunk = (COEF, YZ)
    vmem = pl.BlockSpec(memory_space=pltpu.VMEM)
    smem = pl.BlockSpec(memory_space=pltpu.SMEM)
    owned, head, fgrad = pl.pallas_call(
        functools.partial(kernel, planes, rows_x),
        out_shape=(
            jax.ShapeDtypeStruct((OWN_MOST, COEF, CELLS), f32),
            jax.ShapeDtypeStruct((8, 128), f32),
            jax.ShapeDtypeStruct(feat.shape, bf16),
        ),
        in_specs=[smem, smem, smem] + [vmem] * 6,
        out_specs=(vmem, vmem, vmem),
        scratch_shapes=[
            pltpu.VMEM((tiles, 2 * YZ, TILE), bf16),
            pltpu.VMEM((tiles, 3 * GX, TILE), f32),
            pltpu.VMEM((tiles, 8, TILE), f32),
            pltpu.VMEM((IMG_ROW, ROWS, YZ), f32),
            pltpu.VMEM((2, ROWS, YZ), f32),
            pltpu.VMEM((2, ROWS, YZ), f32),
            pltpu.VMEM((IMG_ROW, ROWS, YZ), f32),
            pltpu.VMEM((IMG_ROW, 2 * USED, 2 * YZ), bf16),
            pltpu.VMEM((OWN_MOST, COEF, CELLS), f32),
            pltpu.VMEM((8, 128), f32),
            pltpu.VMEM((3, feat.shape[0]), f32),
            pltpu.VMEM((3, TILE), f32),
            pltpu.SMEM((images,), jnp.int32),
            pltpu.SMEM((images,), jnp.int32),
            pltpu.SMEM((images,), jnp.int32),
            pltpu.SMEM((planes * OWN_MOST,), jnp.int32),
            pltpu.VMEM((planes, OWN_MOST) + chunk, f32),
            pltpu.VMEM((planes, OWN_MOST) + chunk, f32),
            pltpu.VMEM((rows_x, IMG_ROW) + chunk, f32),
            pltpu.VMEM((groups, IMG_ROW) + chunk, f32),
            pltpu.VMEM((IMG_ROW,) + chunk, f32),
            pltpu.VMEM((planes, IMG_ROW) + chunk, f32),
            pltpu.VMEM((planes, 2) + chunk, f32),
            pltpu.VMEM((planes, 2) + chunk, f32),
            pltpu.VMEM((2,) + chunk, f32),
            pltpu.VMEM((groups + 1, 2) + chunk, f32),
            pltpu.VMEM((planes, OWN_MOST) + chunk, f32),
            pltpu.VMEM((planes, OWN_MOST) + chunk, f32),
            pltpu.VMEM((planes, 8, 128), f32),
            pltpu.VMEM((8, 128), f32),
            pltpu.VMEM((groups, 8, 128), f32),
            pltpu.SemaphoreType.DMA((2,)),
            pltpu.SemaphoreType.DMA((5, planes)),
            pltpu.SemaphoreType.DMA((5, planes)),
            pltpu.SemaphoreType.DMA((3, groups)),
            pltpu.SemaphoreType.DMA((3, groups)),
        ],
        compiler_params=pltpu.CompilerParams(
            collective_id=0, has_side_effects=True, vmem_limit_bytes=48 << 20
        ),
    )(
        ids,
        tile_image,
        bias,
        table,
        cell.reshape(pixels // 128, 128),
        frac,
        feat,
        weight,
        cot,
    )
    return owned, head[0:3, 0 : feat.shape[0]], head[0:3, feat.shape[0]], fgrad


def solution(mesh):
    rows_x = mesh.shape["img"]
    planes = mesh.shape["pix"] // 2
    return jax.shard_map(
        functools.partial(shards, planes, rows_x),
        mesh=mesh,
        in_specs=(
            P(),
            P(("img", "pix"), None, None),
            P(("img", "pix")),
            P(("img", "pix")),
            P(None, ("img", "pix")),
            P(None, ("img", "pix")),
            P(),
            P(),
            P(None, ("img", "pix")),
        ),
        out_specs=(P(("img", "pix"), None, None), P(), P(), P(None, ("img", "pix"))),
        check_vma=False,
    )
```

time: 755 us -> 61.5 us (0.08)
  matrix products: 257 us -> 0 us
  waiting for transfers between devices: 200 us -> 0 us
  other arithmetic: 113 us -> 0 us
  blocking collectives: 63.8 us -> 0 us
  local copies, waits for them, and re-layouts: 69.4 us -> 11.9 us
  Pallas kernels: 0 us -> 48.6 us
  loops' own time: 33.1 us -> 0 us
  between operations: 14.1 us -> 0.66 us
    dot_general x37 -> x0, matrix products: 257 us -> none  [the longest x16 147 us: tile_step(): lax.dot_general(d_coeffs, splat, (((1,), (1,)), ((), ())), precision=lax....]
    psum x2 -> x0, waiting for transfers between devices: 200 us -> none  [the longest x1 132 us: shards(): summed = lax.psum(contrib, ('img', 'pix'))]
    mul x48 -> x0, other arithmetic: 70.6 us -> none  [the longest x32 70.4 us: splat_matrix(): along_x[:, None, None, :] * along_y[None, :, None, :]]
    psum x1 -> x0, blocking collectives: 63.8 us -> none  [shards(): head_grad, bias_grad = lax.psum((head_part, bias_part), ('img', 'pix'))]
    pallas_call x0 -> x1, Pallas kernels: none -> 48.6 us  [shards(): pl.pallas_call(functools.partial(kernel, planes, rows_x), out_shape=(jax....]
    another operation x1 -> x0, loops' own time: 33.1 us -> none  [shards(): lax.scan(tile_step, grads_init, (tile_image, cells_tiled, fracs_tiled, up...]
    dynamic_slice x33 -> x0, local copies, waits for them, and re-layouts: 29.2 us -> none  [the longest x16 17.6 us: tile_step(): lax.dynamic_index_in_dim(step_grids, image_here, 0, keepdims=False)]
    add x97 -> x0, other arithmetic: 13.4 us -> none  [the longest x1 9.56 us: tv_gradient(): summed + (jnp.concatenate([zeros_rim, diffs], axis=axis) - jnp.concatenat...]
  transfers between devices with their start and end apart: 2 -> 0, of which waited for: 2 -> 0; matrix products, arithmetic and copies ran while one was open for 5% -> 0% of each run, Pallas kernels for 0% -> 0%
where the time goes in v1:
time: 61.5 us; the launch traced here: 61.2 us
  Pallas kernels  48.6 us (79%)
  local copies, waits for them, and re-layouts  11.9 us (19%)
  between operations  0.66 us (1%)
    pallas_call x1, Pallas kernels, shards(): pl.pallas_call(functools.partial(kernel, planes, rows_x), out_shape=(jax....  48.6 us
    unnamed x19, local copies, waits for them, and re-layouts  10.7 us
    slice x2, local copies, waits for them, and re-layouts, shards(): return (owned, head[0:3, 0:feat.shape[0]], head[0:3, feat.shape[0]], fgrad)  1.27 us

profile of v1, /device:TPU:1, one launch (start us, length us, event | category | flops | bytes accessed | tf_op | source)
XLA Modules:
  0.0 61.2 jit_solution(4185379149797490636)
XLA Ops:
  0.6 1.6 %copy.15.table_ref = f32[8,12,2048]{2,1,0:T(8,128)S(1)} copy(f32[8,12,2048]{2,0,1:T(8,128)} %param.10) | data formatting | bytes 1572864 | tf_op args[1]
  2.2 0.0 copy-start
  2.2 1.6 %copy-done = bf16[64,16384]{1,0:T(8,128)(2,1)S(1)} copy-done((bf16[64,16384]{1,0:T(8,128)(2,1)S(1)}, bf16[64,16384]{1,0:T(8,128)(2,1)}, u32[]{:S(2)}) %copy-start) | copy-done | bytes 2097176
  3.8 0.0 copy-start.1
  3.8 0.9 %copy-done.1 = f32[3,16384]{1,0:T(4,128)S(1)} copy-done((f32[3,16384]{1,0:T(4,128)S(1)}, f32[3,16384]{1,0:T(4,128)}, u32[]{:S(2)}) %copy-start.1) | copy-done | bytes 196632
  4.8 0.0 copy-start.2
  4.8 0.9 %copy-done.2 = bf16[3,16384]{1,0:T(4,128)(2,1)S(1)} copy-done((bf16[3,16384]{1,0:T(4,128)(2,1)S(1)}, bf16[3,16384]{1,0:T(4,128)(2,1)}, u32[]{:S(2)}) %copy-start.2) | copy-done | bytes 98328
  5.7 0.0 copy-start.3
  5.7 0.8 %copy-done.3 = s32[16384]{0:T(1024)S(1)} copy-done((s32[16384]{0:T(1024)S(1)}, s32[16384]{0:T(1024)}, u32[]{:S(2)}) %copy-start.3) | copy-done | bytes 65560
  6.5 0.0 copy-start.4
  6.5 0.7 %copy-done.4 = bf16[3,64]{1,0:T(4,128)(2,1)S(1)} copy-done((bf16[3,64]{1,0:T(4,128)(2,1)S(1)}, bf16[3,64]{1,0:T(4,128)(2,1)}, u32[]{:S(2)}) %copy-start.4) | copy-done | bytes 408
  7.2 0.0 copy-start.5
  7.2 0.7 %copy-done.5 = s32[16]{0:T(128)S(1)} copy-done((s32[16]{0:T(128)S(1)}, s32[16]{0:T(128)}, u32[]{:S(2)}) %copy-start.5) | copy-done | bytes 88
  7.9 0.0 copy-start.6
  7.9 0.7 %copy-done.6 = s32[16]{0:T(128)S(1)} copy-done((s32[16]{0:T(128)S(1)}, s32[16]{0:T(128)}, u32[]{:S(2)}) %copy-start.6) | copy-done | bytes 88
  8.5 0.0 copy-start.7
  8.5 0.7 %copy-done.7 = f32[3]{0:T(128)S(1)} copy-done((f32[3]{0:T(128)S(1)}, f32[3]{0:T(128)}, u32[]{:S(2)}) %copy-start.7) | copy-done | bytes 36
  9.2 48.6 %shard_map.120 = (f32[2,12,2048]{2,1,0:T(8,128)S(1)}, f32[8,128]{1,0:T(8,128)S(1)}, bf16[64,16384]{1,0:T(8,128)(2,1)S(1)}) custom-call(s32[16]{0:T(128)S(1)} %copy-done.5, s32[16]{0:T(128)S(1)} %copy-done.6, f32[3]{0:T(128)S(1)} %copy-done.7, f32[8,12,2048]{2,1,0:T(8,128)S(1)} %copy.15.table_ref, s32[128,128]{1,0:T(8,128)S(1)} %bitcast.1, ...), custom_call_target="tpu_custom_call" | custom-call | tf_op jit(solution)/shard_map/pallas_call | solution.py:463
  57.8 0.8 %copy.16 = f32[2,12,2048]{2,0,1:T(2,128)} copy(f32[2,12,2048]{2,1,0:T(8,128)S(1)} %get-tuple-element.14) | data formatting | bytes 393216
  58.6 0.7 %slice_reduce_fusion = f32[3]{0:T(128)} fusion(f32[8,128]{1,0:T(8,128)S(1)} %get-tuple-element.8), kind=kLoop, calls=%fused_computation | loop fusion | bytes 24 | tf_op jit(solution)/shard_map/slice | solution.py:524
  59.3 0.6 slice.6
  59.9 1.3 %copy.18 = bf16[64,16384]{1,0:T(8,128)(2,1)} copy(bf16[64,16384]{1,0:T(8,128)(2,1)S(1)} %get-tuple-element.25) | data formatting | bytes 4194304
Async XLA Ops:
  2.2 1.6 %copy-start = (bf16[64,16384]{1,0:T(8,128)(2,1)S(1)}, bf16[64,16384]{1,0:T(8,128)(2,1)}, u32[]{:S(2)}) copy-start(bf16[64,16384]{1,0:T(8,128)(2,1)} %feat_ref.1) | copy-start | bytes 6291460
  3.8 0.9 %copy-start.1 = (f32[3,16384]{1,0:T(4,128)S(1)}, f32[3,16384]{1,0:T(4,128)}, u32[]{:S(2)}) copy-start(f32[3,16384]{1,0:T(4,128)} %frac_ref.1) | copy-start | bytes 589828
  4.8 0.9 %copy-start.2 = (bf16[3,16384]{1,0:T(4,128)(2,1)S(1)}, bf16[3,16384]{1,0:T(4,128)(2,1)}, u32[]{:S(2)}) copy-start(bf16[3,16384]{1,0:T(4,128)(2,1)} %cot_ref.1) | copy-start | bytes 294916
  5.7 0.8 %copy-start.3 = (s32[16384]{0:T(1024)S(1)}, s32[16384]{0:T(1024)}, u32[]{:S(2)}) copy-start(s32[16384]{0:T(1024)} %param.12) | copy-start | bytes 196612
  6.5 0.7 %copy-start.4 = (bf16[3,64]{1,0:T(4,128)(2,1)S(1)}, bf16[3,64]{1,0:T(4,128)(2,1)}, u32[]{:S(2)}) copy-start(bf16[3,64]{1,0:T(4,128)(2,1)} %weight_ref.1) | copy-start | bytes 1156
  7.2 0.7 %copy-start.5 = (s32[16]{0:T(128)S(1)}, s32[16]{0:T(128)}, u32[]{:S(2)}) copy-start(s32[16]{0:T(128)} %ids_ref.1) | copy-start | bytes 196
  7.9 0.7 %copy-start.6 = (s32[16]{0:T(128)S(1)}, s32[16]{0:T(128)}, u32[]{:S(2)}) copy-start(s32[16]{0:T(128)} %tile_ref.1) | copy-start | bytes 196
  8.5 0.7 %copy-start.7 = (f32[3]{0:T(128)S(1)}, f32[3]{0:T(128)}, u32[]{:S(2)}) copy-start(f32[3]{0:T(128)} %bias_ref.1) | copy-start | bytes 40

commit v2 on v1

v2 whole, which is shorter than its diff:
```python
import functools
import math

import jax
import jax.numpy as jnp
from jax import lax
from jax.experimental import pallas as pl
from jax.experimental.pallas import tpu as pltpu
from jax.sharding import PartitionSpec as P

GX = 16
GY = 16
GZ = 8
YZ = GY * GZ
CELLS = GX * YZ
COEF = 12
TILE = 1024
IMG_ROW = 4
OWN_MOST = 2
ROWS = COEF * GX
USED = 9 * GX
VMEM_LIMIT = 40 << 20
SPLAT_FIRST = 10
SLICE_FIRST = 4
SLICE_SECOND = 12
MESH = pl.DeviceIdType.MESH
NT = (((1,), (1,)), ((), ()))


def spread(block):
    return jnp.concatenate(
        [jnp.broadcast_to(block[s : s + 1, :], (8, 128)) for s in range(8)], axis=1
    )


def hat(coord, level, low, high):
    return jnp.where(coord == level, low, jnp.where(coord == level - 1, high, 0.0))


def hops(a, b):
    return min(a % b, -a % b)


def kernel(
    side,
    rows_x,
    ids_any,
    tile_any,
    bias_any,
    table_any,
    cell_any,
    frac_any,
    feat_any,
    weight_any,
    cot_any,
    owned_ref,
    head_ref,
    fgrad_ref,
    ids_ref,
    tile_ref,
    bias_ref,
    table_ref,
    cell_ref,
    frac_ref,
    feat_ref,
    weight_ref,
    cot_ref,
    in_sems,
    splat_ref,
    uax_ref,
    colour_ref,
    half_ref,
    acc_ref,
    sib_ref,
    total_ref,
    grid_f32,
    grid_ref,
    tv_ref,
    stat_ref,
    head_acc,
    bias_acc,
    holder_q,
    holder_g,
    rank_ref,
    dest_ref,
    g1_send,
    g1_recv,
    g2_send,
    g2_recv,
    g3_send,
    g3_recv,
    r1_send,
    r1_recv,
    r2_send,
    r2_recv,
    r3_send,
    r3_recv,
    h1_recv,
    h2_send,
    h2_recv,
    sib_sems,
    plane_ss,
    plane_rs,
    line_ss,
    line_rs,
):
    operands = (
        (ids_any, ids_ref),
        (cell_any, cell_ref),
        (frac_any, frac_ref),
        (feat_any, feat_ref),
        (weight_any, weight_ref),
        (cot_any, cot_ref),
        (tile_any, tile_ref),
        (bias_any, bias_ref),
    )
    fetches = [
        pltpu.make_async_copy(src, dst, in_sems.at[n])
        for n, (src, dst) in enumerate(operands)
    ]
    planes = side * side
    table_fetches = [
        pltpu.make_async_copy(
            table_any.at[:, pl.ds(q * YZ, YZ)],
            table_ref.at[q],
            in_sems.at[len(operands) + q],
        )
        for q in range(planes)
    ]
    for fetch in fetches[:1] + table_fetches + fetches[1:]:
        fetch.start()
    groups = rows_x * 2
    tiles = cell_ref.shape[0] // 8
    images = ids_ref.shape[0]
    held = table_ref.shape[1] // COEF
    my_x = lax.axis_index("img")
    my_pix = lax.axis_index("pix")
    my_q = my_pix // 2
    my_c = my_pix % 2
    my_g = my_x * 2 + my_c
    my_dev = my_x * (planes * 2) + my_pix

    steps = [(dz, dy) for dz in range(side) for dy in range(side)]
    steps = sorted(steps, key=lambda d: -hops(d[0], side) - hops(d[1], side))[:-1]
    my_z, my_y = my_q // side, my_q % side
    plane_q = [(my_z + dz) % side * side + (my_y + dy) % side for dz, dy in steps]
    steps = [(dx, dc) for dx in range(rows_x) for dc in range(2)]
    steps = sorted(steps, key=lambda d: -2 * hops(d[0], rows_x) - d[1])[:-1]
    line_g = [(my_x + dx) % rows_x * 2 + (my_c + dc) % 2 for dx, dc in steps]

    def plane_dev(q):
        return {"img": my_x, "pix": q * 2 + my_c}

    def line_dev(g):
        return {"img": g // 2, "pix": my_q * 2 + g % 2}

    def plane_copy(stage, q, src, dst, slot=None):
        return pltpu.make_async_remote_copy(
            src_ref=src,
            dst_ref=dst,
            send_sem=plane_ss.at[stage, q],
            recv_sem=plane_rs.at[stage, my_q if slot is None else slot],
            device_id=plane_dev(q),
            device_id_type=MESH,
        )

    def line_copy(stage, g, src, dst, slot=None):
        return pltpu.make_async_remote_copy(
            src_ref=src,
            dst_ref=dst,
            send_sem=line_ss.at[stage, g],
            recv_sem=line_rs.at[stage, my_g if slot is None else slot],
            device_id=line_dev(g),
            device_id_type=MESH,
        )

    def plane_send(stage, src, dst):
        for q in plane_q:
            plane_copy(stage, q, src(q), dst.at[my_q]).start()

    def line_send(stage, src, dst):
        for g in line_g:
            line_copy(stage, g, src(g), dst.at[my_g]).start()

    def plane_arrive(stage, buf):
        for q in plane_q:
            plane_copy(stage, q, buf.at[q], buf.at[q], q).wait_recv()

    def line_arrive(stage, buf):
        for g in line_g:
            line_copy(stage, g, buf.at[g], buf.at[g], g).wait_recv()

    barrier = pltpu.get_barrier_semaphore()
    for q in plane_q:
        pl.semaphore_signal(
            barrier, inc=1, device_id=plane_dev(q), device_id_type=MESH
        )
    for g in line_g:
        pl.semaphore_signal(barrier, inc=1, device_id=line_dev(g), device_id_type=MESH)

    fetches[0].wait()
    holders = []
    ranks = []
    for i in range(images):
        holder = ids_ref[i] // held
        rank = jnp.int32(0)
        for other in holders:
            rank = rank + jnp.where(other == holder, 1, 0)
        holders.append(holder)
        ranks.append(rank)
        hp = holder % (planes * 2)
        holder_q[i] = hp // 2
        holder_g[i] = holder // (planes * 2) * 2 + hp % 2
        rank_ref[i] = rank

    own_row = [jnp.int32(0)] * OWN_MOST
    own_has = [jnp.int32(0)] * OWN_MOST
    for i in range(images):
        for s in range(OWN_MOST):
            hit = (holders[i] == my_dev) & (ranks[i] == s)
            own_row[s] = jnp.where(hit, ids_ref[i] % held, own_row[s])
            own_has[s] = jnp.where(hit, 1, own_has[s])

    for fetch in table_fetches:
        fetch.wait()
    for s in range(OWN_MOST):
        for q in range(planes):
            for k in range(3):
                g1_send[q, s * 9 + 3 * k : s * 9 + 3 * k + 3, :] = table_ref[
                    q, pl.ds(4 * k * held + own_row[s], 3, stride=held), :
                ]
    pl.semaphore_wait(barrier, len(plane_q) + len(line_g))
    plane_send(0, lambda q: g1_send.at[q], g1_recv)
    g1_recv[my_q] = g1_send[my_q]

    def find_dest(q, carry):
        dev = my_x * (planes * 2) + q * 2 + my_c
        for s in range(OWN_MOST):
            found = jnp.int32(images)
            for i in range(images):
                found = jnp.where((holders[i] == dev) & (ranks[i] == s), i, found)
            dest_ref[q * OWN_MOST + s] = found
        return carry

    lax.fori_loop(0, planes, find_dest, 0)

    lane = lax.broadcasted_iota(jnp.int32, (COEF, YZ), 1)
    for s in range(OWN_MOST):
        own = [
            table_ref[q, pl.ds(own_row[s], COEF, stride=held), :]
            for q in range(planes)
        ]
        for q in range(planes):
            here = own[q]
            total = jnp.zeros((COEF, YZ), jnp.float32)
            if q > 0:
                total = total + (here - own[q - 1])
            if q < planes - 1:
                total = total - (own[q + 1] - here)
            for step, first, last in (
                (GZ, lane >= GZ, lane < YZ - GZ),
                (1, lane % GZ != 0, lane % GZ != GZ - 1),
            ):
                before = jnp.where(first, here - pltpu.roll(here, step, 1), 0.0)
                after = jnp.where(last, pltpu.roll(here, YZ - step, 1) - here, 0.0)
                total = total + (before - after)
            tv_ref[q, s * COEF : (s + 1) * COEF, :] = jnp.where(
                own_has[s] == 1, total, 0.0
            )

    acc_ref[...] = jnp.zeros_like(acc_ref)
    head_acc[...] = jnp.zeros_like(head_acc)
    bias_acc[...] = jnp.zeros_like(bias_acc)
    for fetch in fetches[1:]:
        fetch.wait()
    weight_f32 = jnp.concatenate(
        [
            weight_ref[...].astype(jnp.float32),
            jnp.zeros((8 - weight_ref.shape[0], weight_ref.shape[1]), jnp.float32),
        ],
        axis=0,
    )
    weight_rows = weight_f32.astype(jnp.bfloat16)
    weight_cols = (
        jnp.concatenate([weight_f32, jnp.zeros_like(weight_f32)], axis=0)
        .T.astype(jnp.bfloat16)
    )
    chan = lax.broadcasted_iota(jnp.int32, (8, TILE), 0)

    def gather_two():
        plane_arrive(0, g1_recv)
        for i in range(images):
            at = i % IMG_ROW * 9
            g2_send[i // IMG_ROW, at : at + 9, :] = jnp.where(
                rank_ref[i] == 0, g1_recv[holder_q[i], 0:9], g1_recv[holder_q[i], 9:18]
            )
        line_send(0, lambda g: g2_send.at[g // 2], g2_recv)
        g2_recv[my_g] = g2_send[my_x]

    def gather_three():
        line_arrive(0, g2_recv)
        for i in range(IMG_ROW):
            at = i * 9
            g3_send[at : at + 9, :] = g2_recv[
                holder_g[my_x * IMG_ROW + i], at : at + 9
            ]
        plane_send(1, lambda q: g3_send, g3_recv)
        g3_recv[my_q] = g3_send[...]

    def splat_tile(t, carry):
        px = pl.ds(pl.multiple_of(t * TILE, TILE), TILE)
        cell = spread(cell_ref[pl.ds(pl.multiple_of(t * 8, 8), 8), :])
        cx = cell >> 7
        cy = (cell >> 3) & (GY - 1)
        cz = cell & (GZ - 1)
        fx = jnp.broadcast_to(frac_ref[0:1, px], (8, TILE))
        fy = jnp.broadcast_to(frac_ref[1:2, px], (8, TILE))
        fz = jnp.broadcast_to(frac_ref[2:3, px], (8, TILE))
        az = hat(cz, chan, 1.0 - fz, fz)
        gy = 1.0 - fy
        for y in range(0, GY, 2):
            pair = jnp.concatenate(
                [hat(cy, y, gy, fy) * az, hat(cy, y + 1, gy, fy) * az], axis=0
            )
            big = pair.astype(jnp.bfloat16)
            rest = (pair - big.astype(jnp.float32)).astype(jnp.bfloat16)
            splat_ref[t, y * GZ : (y + 2) * GZ, :] = big
            splat_ref[t, YZ + y * GZ : YZ + (y + 2) * GZ, :] = rest
        gx = 1.0 - fx
        ax = jnp.concatenate([hat(cx, chan, gx, fx), hat(cx, chan + 8, gx, fx)], axis=0)
        logits = jnp.dot(
            weight_rows, feat_ref[:, px], preferred_element_type=jnp.float32
        )
        bias = jnp.where(
            chan == 0, bias_ref[0], jnp.where(chan == 1, bias_ref[1], bias_ref[2])
        )
        colour = 1.0 / (1.0 + jnp.exp(-(logits + bias)))
        colour_ref[t] = colour
        parts = []
        for k in range(3):
            u = jnp.broadcast_to(cot_ref[k : k + 1, px].astype(jnp.float32), (GX, TILE))
            uax = u * ax
            uax_ref[t, k * GX : (k + 1) * GX, :] = uax
            for j in range(3):
                col = jnp.broadcast_to(colour[j : j + 1, :], (GX, TILE))
                parts.append((uax * col).astype(jnp.bfloat16))
            parts.append(uax.astype(jnp.bfloat16))
        left = jnp.concatenate(parts, axis=0)
        both = lax.dot_general(
            left, splat_ref[t], NT, preferred_element_type=jnp.float32
        )
        grads = both[:, :YZ] + both[:, YZ:]
        image = tile_ref[t]
        for i in range(IMG_ROW):
            acc_ref[i] += jnp.where(image == i, grads, 0.0)

    def slice_tile(t, carry):
        px = pl.ds(pl.multiple_of(t * TILE, TILE), TILE)
        wide = jnp.dot(
            grid_ref[tile_ref[t]], splat_ref[t], preferred_element_type=jnp.float32
        )
        d_colour = jnp.zeros((8, TILE), jnp.float32)
        for j in range(3):
            total = None
            for k in range(3):
                at = (3 * k + j) * GX
                coef = wide[at : at + GX] + wide[USED + at : USED + at + GX]
                term = coef * uax_ref[t, k * GX : (k + 1) * GX, :]
                total = term if total is None else total + term
            whole = jnp.sum(total, axis=0, keepdims=True)
            d_colour = jnp.where(chan == j, whole, d_colour)
        colour = colour_ref[t]
        d_logits = d_colour * colour * (1.0 - colour)
        d_half = jnp.concatenate([d_logits, jnp.zeros_like(d_logits)], axis=0).astype(
            jnp.bfloat16
        )
        half_ref[t] = d_half
        head_acc[...] += lax.dot_general(
            d_half, feat_ref[:, px], NT, preferred_element_type=jnp.float32
        )
        bias_acc[...] += d_logits

    def run(body, first, last):
        def step(n, carry):
            for m in range(2):
                body(2 * n + m, carry)
            return carry

        lax.fori_loop(first // 2, last // 2, step, 0)

    run(splat_tile, 0, SPLAT_FIRST)
    gather_two()
    run(splat_tile, SPLAT_FIRST, tiles)

    sibling = pltpu.make_async_remote_copy(
        src_ref=acc_ref.at[pl.ds(2 * (1 - my_c), 2)],
        dst_ref=sib_ref,
        send_sem=sib_sems.at[0],
        recv_sem=sib_sems.at[1],
        device_id={"img": my_x, "pix": my_q * 2 + 1 - my_c},
        device_id_type=MESH,
    )
    sibling.start()
    gather_three()
    sibling.wait()
    for i in range(2):
        total_ref[i] = acc_ref[2 * my_c + i] + sib_ref[i]
    for q in range(planes):
        for i in range(2):
            r1_send[q, i * COEF : (i + 1) * COEF, :] = total_ref[
                i, pl.ds(q, COEF, stride=GX), :
            ]
    plane_send(2, lambda q: r1_send.at[q], r1_recv)
    r1_recv[my_q] = r1_send[my_q]

    plane_arrive(1, g3_recv)
    for i in range(IMG_ROW):
        for q in range(planes):
            grid_f32[i, pl.ds(q, 9, stride=GX), :] = g3_recv[q, i * 9 : (i + 1) * 9]
    for i in range(IMG_ROW):
        full = grid_f32[i]
        big = full.astype(jnp.bfloat16)
        rest = (full - big.astype(jnp.float32)).astype(jnp.bfloat16)
        grid_ref[i, 0:USED, 0:YZ] = big
        grid_ref[i, 0:USED, YZ : 2 * YZ] = big
        grid_ref[i, USED : 2 * USED, 0:YZ] = rest
        grid_ref[i, USED : 2 * USED, YZ : 2 * YZ] = rest

    def reduce_two():
        plane_arrive(2, r1_recv)
        total = r1_recv[0]
        for q in range(1, planes):
            total = total + r1_recv[q]
        r2_send[...] = total
        line_send(1, lambda g: r2_send, r2_recv)
        r2_recv[my_g] = total
        r2_recv[groups] = jnp.zeros_like(total)

    def reduce_three():
        line_arrive(1, r2_recv)
        for q in range(planes):
            for s in range(OWN_MOST):
                i = dest_ref[q * OWN_MOST + s]
                r3_send[q, s * COEF : (s + 1) * COEF, :] = jnp.where(
                    i % 2 == 0, r2_recv[i // 2, 0:COEF], r2_recv[i // 2, COEF:]
                )
        plane_send(3, lambda q: r3_send.at[q], r3_recv)
        r3_recv[my_q] = r3_send[my_q]

    run(slice_tile, 0, SLICE_FIRST)
    reduce_two()
    run(slice_tile, SLICE_FIRST, SLICE_SECOND)
    reduce_three()
    run(slice_tile, SLICE_SECOND, tiles)

    bias_sum = jnp.sum(bias_acc[...], axis=1, keepdims=True)
    where_bias = lax.broadcasted_iota(jnp.int32, (8, 128), 0)
    on_lane = lax.broadcasted_iota(jnp.int32, (8, 128), 1)
    bias_row = jnp.sum(
        jnp.where(where_bias == on_lane, bias_sum, 0.0), axis=0, keepdims=True
    )
    head_rows = jnp.concatenate(
        [head_acc[0:8, :], jnp.zeros((8, 128 - head_acc.shape[1]), jnp.float32)], axis=1
    )
    stat_ref[...] = jnp.where(where_bias == 3, bias_row, head_rows)
    plane_send(4, lambda q: stat_ref, h1_recv)
    h1_recv[my_q] = stat_ref[...]

    def feature_tile(t, carry):
        px = pl.ds(pl.multiple_of(t * TILE, TILE), TILE)
        fgrad_ref[:, px] = jnp.dot(
            weight_cols, half_ref[t], preferred_element_type=jnp.float32
        ).astype(jnp.bfloat16)

    run(feature_tile, 0, tiles)
    plane_arrive(4, h1_recv)
    total = h1_recv[0]
    for q in range(1, planes):
        total = total + h1_recv[q]
    h2_send[...] = total
    line_send(2, lambda g: h2_send, h2_recv)
    h2_recv[my_g] = total
    plane_arrive(3, r3_recv)
    for q in range(planes):
        for s in range(OWN_MOST):
            rows = slice(s * COEF, (s + 1) * COEF)
            owned_ref[:, s, q * YZ : (q + 1) * YZ] = r3_recv[q, rows] + tv_ref[q, rows]
    line_arrive(2, h2_recv)
    total = h2_recv[0]
    for g in range(1, groups):
        total = total + h2_recv[g]
    head_ref[...] = total

    for q in plane_q:
        plane_copy(0, q, g1_send.at[q], g1_recv.at[my_q]).wait_send()
        plane_copy(1, q, g3_send, g3_recv.at[my_q]).wait_send()
        plane_copy(2, q, r1_send.at[q], r1_recv.at[my_q]).wait_send()
        plane_copy(3, q, r3_send.at[q], r3_recv.at[my_q]).wait_send()
        plane_copy(4, q, stat_ref, h1_recv.at[my_q]).wait_send()
    for g in line_g:
        line_copy(0, g, g2_send.at[g // 2], g2_recv.at[my_g]).wait_send()
        line_copy(1, g, r2_send, r2_recv.at[my_g]).wait_send()
        line_copy(2, g, h2_send, h2_recv.at[my_g]).wait_send()


def finish(owned_in, stat_in, fgrad_in, owned_ref, head_ref, bias_ref, fgrad_ref, sems):
    copies = [
        pltpu.make_async_copy(fgrad_in, fgrad_ref, sems.at[0]),
        pltpu.make_async_copy(owned_in, owned_ref, sems.at[1]),
    ]
    for copy in copies:
        copy.start()
    head_ref[...] = stat_in[0 : head_ref.shape[0], 0 : head_ref.shape[1]]
    bias_ref[...] = stat_in[3, 0 : bias_ref.shape[0]]
    for copy in copies:
        copy.wait()


def shards(side, rows_x, ids, table, tile_image, cell, frac, feat, weight, bias, cot):
    pixels = cell.shape[0]
    tiles = pixels // TILE
    planes = side * side
    groups = rows_x * 2
    images = ids.shape[0]
    f32, bf16, i32 = jnp.float32, jnp.bfloat16, jnp.int32
    vmem = pl.BlockSpec(memory_space=pltpu.VMEM)
    hbm = pl.BlockSpec(memory_space=pltpu.HBM)
    table_rows = jnp.transpose(table, (1, 0, 2)).reshape(-1, CELLS)
    cell_rows = cell.reshape(pixels // 128, 128)
    owned, stat, fgrad = pl.pallas_call(
        functools.partial(kernel, side, rows_x),
        out_shape=(
            jax.ShapeDtypeStruct((COEF, OWN_MOST, CELLS), f32),
            jax.ShapeDtypeStruct((8, 128), f32),
            jax.ShapeDtypeStruct(feat.shape, bf16),
        ),
        in_specs=[hbm] * 9,
        out_specs=(vmem, vmem, vmem),
        scratch_shapes=[
            pltpu.SMEM(ids.shape, i32),
            pltpu.SMEM(tile_image.shape, i32),
            pltpu.SMEM(bias.shape, f32),
            pltpu.VMEM((planes, table_rows.shape[0], YZ), f32),
            pltpu.VMEM(cell_rows.shape, i32),
            pltpu.VMEM(frac.shape, f32),
            pltpu.VMEM(feat.shape, bf16),
            pltpu.VMEM(weight.shape, bf16),
            pltpu.VMEM(cot.shape, bf16),
            pltpu.SemaphoreType.DMA((8 + planes,)),
            pltpu.VMEM((tiles, 2 * YZ, TILE), bf16),
            pltpu.VMEM((tiles, 3 * GX, TILE), f32),
            pltpu.VMEM((tiles, 8, TILE), f32),
            pltpu.VMEM((tiles, 16, TILE), bf16),
            pltpu.VMEM((IMG_ROW, ROWS, YZ), f32),
            pltpu.VMEM((2, ROWS, YZ), f32),
            pltpu.VMEM((2, ROWS, YZ), f32),
            pltpu.VMEM((IMG_ROW, USED, YZ), f32),
            pltpu.VMEM((IMG_ROW, 2 * USED, 2 * YZ), bf16),
            pltpu.VMEM((planes, OWN_MOST * COEF, YZ), f32),
            pltpu.VMEM((8, 128), f32),
            pltpu.VMEM((16, feat.shape[0]), f32),
            pltpu.VMEM((8, TILE), f32),
            pltpu.SMEM((images,), i32),
            pltpu.SMEM((images,), i32),
            pltpu.SMEM((images,), i32),
            pltpu.SMEM((planes * OWN_MOST,), i32),
            pltpu.VMEM((planes, OWN_MOST * 9, YZ), f32),
            pltpu.VMEM((planes, OWN_MOST * 9, YZ), f32),
            pltpu.VMEM((rows_x, IMG_ROW * 9, YZ), f32),
            pltpu.VMEM((groups, IMG_ROW * 9, YZ), f32),
            pltpu.VMEM((IMG_ROW * 9, YZ), f32),
            pltpu.VMEM((planes, IMG_ROW * 9, YZ), f32),
            pltpu.VMEM((planes, 2 * COEF, YZ), f32),
            pltpu.VMEM((planes, 2 * COEF, YZ), f32),
            pltpu.VMEM((2 * COEF, YZ), f32),
            pltpu.VMEM((groups + 1, 2 * COEF, YZ), f32),
            pltpu.VMEM((planes, OWN_MOST * COEF, YZ), f32),
            pltpu.VMEM((planes, OWN_MOST * COEF, YZ), f32),
            pltpu.VMEM((planes, 8, 128), f32),
            pltpu.VMEM((8, 128), f32),
            pltpu.VMEM((groups, 8, 128), f32),
            pltpu.SemaphoreType.DMA((2,)),
            pltpu.SemaphoreType.DMA((5, planes)),
            pltpu.SemaphoreType.DMA((5, planes)),
            pltpu.SemaphoreType.DMA((3, groups)),
            pltpu.SemaphoreType.DMA((3, groups)),
        ],
        compiler_params=pltpu.CompilerParams(
            collective_id=0, has_side_effects=True, vmem_limit_bytes=VMEM_LIMIT
        ),
    )(
        *(
            pltpu.with_memory_space_constraint(operand, pltpu.HBM)
            for operand in (
                ids,
                tile_image,
                bias,
                table_rows,
                cell_rows,
                frac,
                feat,
                weight,
                cot,
            )
        )
    )
    owned, head, bias_grad, fgrad = pl.pallas_call(
        finish,
        out_shape=(
            jax.ShapeDtypeStruct((COEF, OWN_MOST, CELLS), f32),
            jax.ShapeDtypeStruct(weight.shape, f32),
            jax.ShapeDtypeStruct(bias.shape, f32),
            jax.ShapeDtypeStruct(feat.shape, bf16),
        ),
        in_specs=[vmem, vmem, vmem],
        out_specs=(hbm, vmem, vmem, hbm),
        scratch_shapes=[pltpu.SemaphoreType.DMA((2,))],
        compiler_params=pltpu.CompilerParams(vmem_limit_bytes=16 << 20),
    )(owned, stat, fgrad)
    return jnp.transpose(owned, (1, 0, 2)), head, bias_grad, fgrad


def solution(mesh):
    rows_x = mesh.shape["img"]
    side = math.isqrt(mesh.shape["pix"] // 2)
    return jax.shard_map(
        functools.partial(shards, side, rows_x),
        mesh=mesh,
        in_specs=(
            P(),
            P(("img", "pix"), None, None),
            P(("img", "pix")),
            P(("img", "pix")),
            P(None, ("img", "pix")),
            P(None, ("img", "pix")),
            P(),
            P(),
            P(None, ("img", "pix")),
        ),
        out_specs=(P(("img", "pix"), None, None), P(), P(), P(None, ("img", "pix"))),
        check_vma=False,
    )
```

time: 61.5 us -> 44.6 us (0.73)
  local copies, waits for them, and re-layouts: 11.9 us -> 0 us
  Pallas kernels: 48.6 us -> 43.8 us
    unnamed x19 -> x0, local copies, waits for them, and re-layouts: 10.7 us -> none
    pallas_call x1 -> x2, Pallas kernels: 48.6 us -> 43.8 us  [the longest x1 41.9 us: shards(): pl.pallas_call(functools.partial(kernel, side, rows_x), out_shape=(jax.Sh...]
    slice x2 -> x0, local copies, waits for them, and re-layouts: 1.27 us -> none  [shards(): return (owned, head[0:3, 0:feat.shape[0]], head[0:3, feat.shape[0]], fgrad)]
where the time goes in v2:
time: 44.6 us; the launch traced here: 44.5 us
  Pallas kernels  43.8 us (98%)
  between operations  0.64 us (1%)
    pallas_call x1, Pallas kernels, shards(): pl.pallas_call(functools.partial(kernel, side, rows_x), out_shape=(jax.Sh...  41.9 us
    pallas_call x1, Pallas kernels, shards(): pl.pallas_call(finish, out_shape=(jax.ShapeDtypeStruct((COEF, OWN_MOST, C...  1.96 us

profile of v2, /device:TPU:1, one launch (start us, length us, event | category | flops | bytes accessed | tf_op | source)
XLA Modules:
  0.0 44.5 jit_solution(7139022360861341012)
XLA Ops:
  0.6 41.9 %shard_map.120 = (f32[12,2,2048]{2,1,0:T(2,128)S(1)}, f32[8,128]{1,0:T(8,128)S(1)}, bf16[64,16384]{1,0:T(8,128)(2,1)S(1)}) custom-call(s32[16]{0:T(128)} %ids_any.1, s32[16]{0:T(128)} %tile_any.1, f32[3]{0:T(128)} %bias_any.1, f32[96,2048]{1,0:T(8,128)} %bitcast.5, s32[128,128]{1,0:T(8,128)} %bitcast.6, f32[3,16384]{1,0:T(4,128)} %frac_any.1, ...), custom_call_target="tpu_custom_call" | custom-call | tf_op jit(solution)/shard_map/pallas_call | solution.py:530
  42.5 2.0 %shard_map.121 = (f32[12,2,2048]{2,1,0:T(2,128)}, f32[3,64]{1,0:T(4,128)}, f32[3]{0:T(128)}, bf16[64,16384]{1,0:T(8,128)(2,1)}) custom-call(f32[12,2,2048]{2,1,0:T(2,128)S(1)} %get-tuple-element.11.owned_in, f32[8,128]{1,0:T(8,128)S(1)} %get-tuple-element.12.stat_in, bf16[64,16384]{1,0:T(8,128)(2,1)S(1)} %get-tuple-element.13.fgrad_in), custom_call_target="tpu_custom_call" | custom-call | tf_op jit(solution)/shard_map/pallas_call | solution.py:607

commit v3 on v2

v3 whole, which is shorter than its diff:
```python
import functools
import math

import jax
import jax.numpy as jnp
from jax import lax
from jax.experimental import pallas as pl
from jax.experimental.pallas import tpu as pltpu
from jax.sharding import PartitionSpec as P

GX = 16
GY = 16
GZ = 8
YZ = GY * GZ
CELLS = GX * YZ
COEF = 12
TILE = 1024
IMG_ROW = 4
OWN_MOST = 2
ROWS = COEF * GX
USED = 9 * GX
VMEM_LIMIT = 40 << 20
SPLAT_UNROLL = 8
SLICE_UNROLL = 16
FEATURE_UNROLL = 8
MESH = pl.DeviceIdType.MESH
NT = (((1,), (1,)), ((), ()))


def spread(block):
    return jnp.concatenate(
        [jnp.broadcast_to(block[s : s + 1, :], (8, 128)) for s in range(8)], axis=1
    )


def hat(coord, level, low, high):
    return jnp.where(coord == level, low, jnp.where(coord == level - 1, high, 0.0))


def hops(a, b):
    return min(a % b, -a % b)


def kernel(
    side,
    rows_x,
    ids_any,
    tile_any,
    bias_any,
    table_any,
    cell_any,
    frac_any,
    feat_any,
    weight_any,
    cot_any,
    owned_ref,
    head_ref,
    fgrad_ref,
    ids_ref,
    tile_ref,
    bias_ref,
    table_ref,
    cell_ref,
    frac_ref,
    feat_ref,
    weight_ref,
    cot_ref,
    in_sems,
    splat_ref,
    uax_ref,
    colour_ref,
    half_ref,
    acc_ref,
    sib_ref,
    total_ref,
    grid_f32,
    grid_ref,
    tv_ref,
    stat_ref,
    bias_acc,
    holder_q,
    holder_g,
    rank_ref,
    dest_ref,
    g1_send,
    g1_recv,
    g2_send,
    g2_recv,
    g3_send,
    g3_recv,
    r1_send,
    r1_recv,
    r2_send,
    r2_recv,
    r3_send,
    r3_recv,
    h1_recv,
    head_sems,
    sib_sems,
    plane_ss,
    plane_rs,
    line_ss,
    line_rs,
):
    operands = (
        (ids_any, ids_ref),
        (cell_any, cell_ref),
        (frac_any, frac_ref),
        (feat_any, feat_ref),
        (weight_any, weight_ref),
        (cot_any, cot_ref),
        (tile_any, tile_ref),
        (bias_any, bias_ref),
    )
    fetches = [
        pltpu.make_async_copy(src, dst, in_sems.at[n])
        for n, (src, dst) in enumerate(operands)
    ]
    planes = side * side
    table_fetches = [
        pltpu.make_async_copy(
            table_any.at[:, pl.ds(q * YZ, YZ)],
            table_ref.at[q],
            in_sems.at[len(operands) + q],
        )
        for q in range(planes)
    ]
    groups = rows_x * 2
    tiles = cell_ref.shape[0] // 8
    images = ids_ref.shape[0]
    held = table_ref.shape[1] // COEF
    my_x = lax.axis_index("img")
    my_pix = lax.axis_index("pix")
    my_q = my_pix // 2
    my_c = my_pix % 2
    my_g = my_x * 2 + my_c
    my_dev = my_x * (planes * 2) + my_pix

    steps = [(dz, dy) for dz in range(side) for dy in range(side)]
    steps = sorted(steps, key=lambda d: -hops(d[0], side) - hops(d[1], side))[:-1]
    my_z, my_y = my_q // side, my_q % side
    plane_q = [(my_z + dz) % side * side + (my_y + dy) % side for dz, dy in steps]
    steps = [(dx, dc) for dx in range(rows_x) for dc in range(2)]
    steps = sorted(steps, key=lambda d: -2 * hops(d[0], rows_x) - d[1])[:-1]
    line_g = [(my_x + dx) % rows_x * 2 + (my_c + dc) % 2 for dx, dc in steps]

    def plane_dev(q):
        return {"img": my_x, "pix": q * 2 + my_c}

    def line_dev(g):
        return {"img": g // 2, "pix": my_q * 2 + g % 2}

    def plane_copy(stage, q, src, dst, slot=None):
        return pltpu.make_async_remote_copy(
            src_ref=src,
            dst_ref=dst,
            send_sem=plane_ss.at[stage, q],
            recv_sem=plane_rs.at[stage, my_q if slot is None else slot],
            device_id=plane_dev(q),
            device_id_type=MESH,
        )

    def line_copy(stage, g, src, dst, slot=None):
        return pltpu.make_async_remote_copy(
            src_ref=src,
            dst_ref=dst,
            send_sem=line_ss.at[stage, g],
            recv_sem=line_rs.at[stage, my_g if slot is None else slot],
            device_id=line_dev(g),
            device_id_type=MESH,
        )

    steps = [
        (dx, dz, dy, dc)
        for dx in range(rows_x)
        for dz in range(side)
        for dy in range(side)
        for dc in range(2)
    ]
    far = [hops(dx, rows_x) + hops(dz, side) + hops(dy, side) for dx, dz, dy, _ in steps]
    order = sorted(range(len(steps)), key=lambda n: -2 * far[n] - steps[n][3])[:-1]
    head_devs = []
    for dx, dz, dy, dc in [steps[n] for n in order]:
        q = (my_z + dz) % side * side + (my_y + dy) % side
        head_devs.append(
            {"img": (my_x + dx) % rows_x, "pix": q * 2 + (my_c + dc) % 2}
        )

    def head_copy(dev):
        return pltpu.make_async_remote_copy(
            src_ref=stat_ref,
            dst_ref=h1_recv.at[my_dev],
            send_sem=head_sems.at[0],
            recv_sem=head_sems.at[1],
            device_id=dev,
            device_id_type=MESH,
        )

    def plane_send(stage, src, dst):
        for q in plane_q:
            plane_copy(stage, q, src(q), dst.at[my_q]).start()

    def line_send(stage, src, dst):
        for g in line_g:
            line_copy(stage, g, src(g), dst.at[my_g]).start()

    def plane_arrive(stage, buf):
        for q in plane_q:
            plane_copy(stage, q, buf.at[q], buf.at[q], q).wait_recv()

    def line_arrive(stage, buf):
        for g in line_g:
            line_copy(stage, g, buf.at[g], buf.at[g], g).wait_recv()

    barrier = pltpu.get_barrier_semaphore()
    for q in plane_q:
        pl.semaphore_signal(
            barrier, inc=1, device_id=plane_dev(q), device_id_type=MESH
        )
    for g in line_g:
        pl.semaphore_signal(barrier, inc=1, device_id=line_dev(g), device_id_type=MESH)

    for fetch in fetches[:1] + table_fetches + fetches[1:]:
        fetch.start()

    acc_ref[...] = jnp.zeros_like(acc_ref)
    bias_acc[...] = jnp.zeros_like(bias_acc)
    fetches[0].wait()
    holders = []
    ranks = []
    for i in range(images):
        holder = ids_ref[i] // held
        rank = jnp.int32(0)
        for other in holders:
            rank = rank + jnp.where(other == holder, 1, 0)
        holders.append(holder)
        ranks.append(rank)
        hp = holder % (planes * 2)
        holder_q[i] = hp // 2
        holder_g[i] = holder // (planes * 2) * 2 + hp % 2
        rank_ref[i] = rank

    own_row = [jnp.int32(0)] * OWN_MOST
    own_has = [jnp.int32(0)] * OWN_MOST
    for i in range(images):
        for s in range(OWN_MOST):
            hit = (holders[i] == my_dev) & (ranks[i] == s)
            own_row[s] = jnp.where(hit, ids_ref[i] % held, own_row[s])
            own_has[s] = jnp.where(hit, 1, own_has[s])

    for fetch in table_fetches:
        fetch.wait()
    for s in range(OWN_MOST):
        for q in range(planes):
            for k in range(3):
                g1_send[q, s * 9 + 3 * k : s * 9 + 3 * k + 3, :] = table_ref[
                    q, pl.ds(4 * k * held + own_row[s], 3, stride=held), :
                ]
    pl.semaphore_wait(barrier, len(plane_q) + len(line_g))
    plane_send(0, lambda q: g1_send.at[q], g1_recv)
    g1_recv[my_q] = g1_send[my_q]

    for fetch in fetches[1:]:
        fetch.wait()
    weight_f32 = jnp.concatenate(
        [
            weight_ref[...].astype(jnp.float32),
            jnp.zeros((8 - weight_ref.shape[0], weight_ref.shape[1]), jnp.float32),
        ],
        axis=0,
    )
    weight_rows = weight_f32.astype(jnp.bfloat16)
    weight_cols = (
        jnp.concatenate([weight_f32, jnp.zeros_like(weight_f32)], axis=0)
        .T.astype(jnp.bfloat16)
    )
    chan = lax.broadcasted_iota(jnp.int32, (8, TILE), 0)

    def gather_two():
        plane_arrive(0, g1_recv)
        for i in range(images):
            at = i % IMG_ROW * 9
            g2_send[i // IMG_ROW, at : at + 9, :] = jnp.where(
                rank_ref[i] == 0, g1_recv[holder_q[i], 0:9], g1_recv[holder_q[i], 9:18]
            )
        line_send(0, lambda g: g2_send.at[g // 2], g2_recv)
        g2_recv[my_g] = g2_send[my_x]

    def gather_three():
        line_arrive(0, g2_recv)
        for i in range(IMG_ROW):
            at = i * 9
            g3_send[at : at + 9, :] = g2_recv[
                holder_g[my_x * IMG_ROW + i], at : at + 9
            ]
        plane_send(1, lambda q: g3_send, g3_recv)
        g3_recv[my_q] = g3_send[...]

    def splat_tile(t):
        px = pl.ds(pl.multiple_of(t * TILE, TILE), TILE)
        cell = spread(cell_ref[pl.ds(pl.multiple_of(t * 8, 8), 8), :])
        cx = cell >> 7
        cy = (cell >> 3) & (GY - 1)
        cz = cell & (GZ - 1)
        fx = jnp.broadcast_to(frac_ref[0:1, px], (8, TILE))
        fy = jnp.broadcast_to(frac_ref[1:2, px], (8, TILE))
        fz = jnp.broadcast_to(frac_ref[2:3, px], (8, TILE))
        az = hat(cz, chan, 1.0 - fz, fz)
        gy = 1.0 - fy
        for y in range(0, GY, 2):
            pair = jnp.concatenate(
                [hat(cy, y, gy, fy) * az, hat(cy, y + 1, gy, fy) * az], axis=0
            )
            big = pair.astype(jnp.bfloat16)
            rest = (pair - big.astype(jnp.float32)).astype(jnp.bfloat16)
            splat_ref[t, y * GZ : (y + 2) * GZ, :] = big
            splat_ref[t, YZ + y * GZ : YZ + (y + 2) * GZ, :] = rest
        gx = 1.0 - fx
        ax = jnp.concatenate([hat(cx, chan, gx, fx), hat(cx, chan + 8, gx, fx)], axis=0)
        logits = jnp.dot(
            weight_rows, feat_ref[:, px], preferred_element_type=jnp.float32
        )
        bias = jnp.where(
            chan == 0, bias_ref[0], jnp.where(chan == 1, bias_ref[1], bias_ref[2])
        )
        colour = 1.0 / (1.0 + jnp.exp(-(logits + bias)))
        colour_ref[t] = colour
        parts = []
        for k in range(3):
            u = jnp.broadcast_to(cot_ref[k : k + 1, px].astype(jnp.float32), (GX, TILE))
            uax = u * ax
            uax_ref[t, k * GX : (k + 1) * GX, :] = uax
            for j in range(3):
                col = jnp.broadcast_to(colour[j : j + 1, :], (GX, TILE))
                parts.append((uax * col).astype(jnp.bfloat16))
            parts.append(uax.astype(jnp.bfloat16))
        left = jnp.concatenate(parts, axis=0)
        both = lax.dot_general(
            left, splat_ref[t], NT, preferred_element_type=jnp.float32
        )
        grads = both[:, :YZ] + both[:, YZ:]
        image = tile_ref[t]
        for i in range(IMG_ROW):
            acc_ref[i] += jnp.where(image == i, grads, 0.0)

    def slice_tile(t):
        px = pl.ds(pl.multiple_of(t * TILE, TILE), TILE)
        wide = jnp.dot(
            grid_ref[tile_ref[t]], splat_ref[t], preferred_element_type=jnp.float32
        )
        d_colour = jnp.zeros((8, TILE), jnp.float32)
        for j in range(3):
            total = None
            for k in range(3):
                at = (3 * k + j) * GX
                coef = wide[at : at + GX] + wide[USED + at : USED + at + GX]
                term = coef * uax_ref[t, k * GX : (k + 1) * GX, :]
                total = term if total is None else total + term
            whole = jnp.sum(total, axis=0, keepdims=True)
            d_colour = jnp.where(chan == j, whole, d_colour)
        colour = colour_ref[t]
        d_logits = d_colour * colour * (1.0 - colour)
        d_half = jnp.concatenate([d_logits, jnp.zeros_like(d_logits)], axis=0).astype(
            jnp.bfloat16
        )
        half_ref[:, px] = d_half
        bias_acc[...] += d_logits

    def run(body, unroll):
        def step(n, carry):
            for m in range(unroll):
                body(unroll * n + m)
            return carry

        lax.fori_loop(0, tiles // unroll, step, 0)

    run(splat_tile, SPLAT_UNROLL)

    sibling = pltpu.make_async_remote_copy(
        src_ref=acc_ref.at[pl.ds(2 * (1 - my_c), 2)],
        dst_ref=sib_ref,
        send_sem=sib_sems.at[0],
        recv_sem=sib_sems.at[1],
        device_id={"img": my_x, "pix": my_q * 2 + 1 - my_c},
        device_id_type=MESH,
    )
    sibling.start()
    gather_two()
    sibling.wait()
    for i in range(2):
        total_ref[i] = acc_ref[2 * my_c + i] + sib_ref[i]
    for q in range(planes):
        for i in range(2):
            r1_send[q, i * COEF : (i + 1) * COEF, :] = total_ref[
                i, pl.ds(q, COEF, stride=GX), :
            ]
    plane_send(2, lambda q: r1_send.at[q], r1_recv)
    r1_recv[my_q] = r1_send[my_q]

    gather_three()

    def find_dest(q, carry):
        dev = my_x * (planes * 2) + q * 2 + my_c
        for s in range(OWN_MOST):
            found = jnp.int32(images)
            for i in range(images):
                found = jnp.where((holders[i] == dev) & (ranks[i] == s), i, found)
            dest_ref[q * OWN_MOST + s] = found
        return carry

    lax.fori_loop(0, planes, find_dest, 0)

    lane = lax.broadcasted_iota(jnp.int32, (COEF, YZ), 1)
    for s in range(OWN_MOST):
        own = [
            table_ref[q, pl.ds(own_row[s], COEF, stride=held), :]
            for q in range(planes)
        ]
        for q in range(planes):
            here = own[q]
            total = jnp.zeros((COEF, YZ), jnp.float32)
            if q > 0:
                total = total + (here - own[q - 1])
            if q < planes - 1:
                total = total - (own[q + 1] - here)
            for step, first, last in (
                (GZ, lane >= GZ, lane < YZ - GZ),
                (1, lane % GZ != 0, lane % GZ != GZ - 1),
            ):
                before = jnp.where(first, here - pltpu.roll(here, step, 1), 0.0)
                after = jnp.where(last, pltpu.roll(here, YZ - step, 1) - here, 0.0)
                total = total + (before - after)
            tv_ref[q, s * COEF : (s + 1) * COEF, :] = jnp.where(
                own_has[s] == 1, total, 0.0
            )

    def reduce_two():
        plane_arrive(2, r1_recv)
        total = r1_recv[0]
        for q in range(1, planes):
            total = total + r1_recv[q]
        r2_send[...] = total
        line_send(1, lambda g: r2_send, r2_recv)
        r2_recv[my_g] = total
        r2_recv[groups] = jnp.zeros_like(total)

    def reduce_three():
        line_arrive(1, r2_recv)
        for q in range(planes):
            for s in range(OWN_MOST):
                i = dest_ref[q * OWN_MOST + s]
                r3_send[q, s * COEF : (s + 1) * COEF, :] = jnp.where(
                    i % 2 == 0, r2_recv[i // 2, 0:COEF], r2_recv[i // 2, COEF:]
                )
        plane_send(3, lambda q: r3_send.at[q], r3_recv)
        r3_recv[my_q] = r3_send[my_q]

    reduce_two()
    plane_arrive(1, g3_recv)
    for i in range(IMG_ROW):
        for q in range(planes):
            grid_f32[i, pl.ds(q, 9, stride=GX), :] = g3_recv[q, i * 9 : (i + 1) * 9]
    for i in range(IMG_ROW):
        full = grid_f32[i]
        big = full.astype(jnp.bfloat16)
        rest = (full - big.astype(jnp.float32)).astype(jnp.bfloat16)
        grid_ref[i, 0:USED, 0:YZ] = big
        grid_ref[i, 0:USED, YZ : 2 * YZ] = big
        grid_ref[i, USED : 2 * USED, 0:YZ] = rest
        grid_ref[i, USED : 2 * USED, YZ : 2 * YZ] = rest

    run(slice_tile, SLICE_UNROLL)

    head = lax.dot_general(
        half_ref[...], feat_ref[...], NT, preferred_element_type=jnp.float32
    )
    bias_sum = jnp.sum(bias_acc[...], axis=1, keepdims=True)
    on_row = lax.broadcasted_iota(jnp.int32, (8, head.shape[1]), 0)
    on_lane = lax.broadcasted_iota(jnp.int32, (8, head.shape[1]), 1)
    bias_row = jnp.sum(
        jnp.where(on_row == on_lane, bias_sum, 0.0), axis=0, keepdims=True
    )
    stat_ref[0:1, :] = jnp.concatenate([head[0:1], head[1:2]], axis=1)
    stat_ref[1:2, :] = jnp.concatenate([head[2:3], bias_row], axis=1)
    own_stat = pltpu.make_async_copy(stat_ref, h1_recv.at[my_dev], head_sems.at[1])
    own_stat.start()
    for dev in head_devs:
        head_copy(dev).start()
    reduce_three()

    def feature_tile(t):
        px = pl.ds(pl.multiple_of(t * TILE, TILE), TILE)
        fgrad_ref[:, px] = jnp.dot(
            weight_cols, half_ref[:, px], preferred_element_type=jnp.float32
        ).astype(jnp.bfloat16)

    run(feature_tile, FEATURE_UNROLL)
    plane_arrive(3, r3_recv)
    for q in range(planes):
        for s in range(OWN_MOST):
            rows = slice(s * COEF, (s + 1) * COEF)
            owned_ref[:, s, q * YZ : (q + 1) * YZ] = r3_recv[q, rows] + tv_ref[q, rows]
    pltpu.make_async_copy(h1_recv, h1_recv, head_sems.at[1]).wait()
    head_ref[...] = jnp.sum(h1_recv[...], axis=0)

    for q in plane_q:
        plane_copy(0, q, g1_send.at[q], g1_recv.at[my_q]).wait_send()
        plane_copy(1, q, g3_send, g3_recv.at[my_q]).wait_send()
        plane_copy(2, q, r1_send.at[q], r1_recv.at[my_q]).wait_send()
        plane_copy(3, q, r3_send.at[q], r3_recv.at[my_q]).wait_send()
    for g in line_g:
        line_copy(0, g, g2_send.at[g // 2], g2_recv.at[my_g]).wait_send()
        line_copy(1, g, r2_send, r2_recv.at[my_g]).wait_send()
    sent = h1_recv.at[pl.ds(0, len(head_devs))]
    pltpu.make_async_copy(sent, sent, head_sems.at[0]).wait()


def finish(
    owned_in,
    stat_in,
    fgrad_in,
    owned_out,
    head_out,
    bias_out,
    fgrad_out,
    head_ref,
    bias_ref,
    sems,
):
    parts = 4
    rows = fgrad_in.shape[0] // parts
    copies = [
        (fgrad_in.at[pl.ds(n * rows, rows)], fgrad_out.at[pl.ds(n * rows, rows)])
        for n in range(parts)
    ]
    copies += [(owned_in, owned_out), (head_ref, head_out), (bias_ref, bias_out)]
    copies = [
        pltpu.make_async_copy(src, dst, sems.at[n])
        for n, (src, dst) in enumerate(copies)
    ]
    for copy in copies[:-2]:
        copy.start()
    width = head_ref.shape[1]
    head_ref[0:1, :] = stat_in[0:1, 0:width]
    head_ref[1:2, :] = stat_in[0:1, width : 2 * width]
    head_ref[2:3, :] = stat_in[1:2, 0:width]
    bias_ref[...] = stat_in[1, width : width + bias_ref.shape[0]]
    for copy in copies[-2:]:
        copy.start()
    for copy in copies:
        copy.wait()


def shards(side, rows_x, ids, table, tile_image, cell, frac, feat, weight, bias, cot):
    pixels = cell.shape[0]
    tiles = pixels // TILE
    planes = side * side
    groups = rows_x * 2
    images = ids.shape[0]
    f32, bf16, i32 = jnp.float32, jnp.bfloat16, jnp.int32
    vmem = pl.BlockSpec(memory_space=pltpu.VMEM)
    hbm = pl.BlockSpec(memory_space=pltpu.HBM)
    table_rows = jnp.transpose(table, (1, 0, 2)).reshape(-1, CELLS)
    cell_rows = cell.reshape(pixels // 128, 128)
    owned, stat, fgrad = pl.pallas_call(
        functools.partial(kernel, side, rows_x),
        out_shape=(
            jax.ShapeDtypeStruct((COEF, OWN_MOST, CELLS), f32),
            jax.ShapeDtypeStruct((2, 128), f32),
            jax.ShapeDtypeStruct(feat.shape, bf16),
        ),
        in_specs=[hbm] * 9,
        out_specs=(vmem, vmem, vmem),
        scratch_shapes=[
            pltpu.SMEM(ids.shape, i32),
            pltpu.SMEM(tile_image.shape, i32),
            pltpu.SMEM(bias.shape, f32),
            pltpu.VMEM((planes, table_rows.shape[0], YZ), f32),
            pltpu.VMEM(cell_rows.shape, i32),
            pltpu.VMEM(frac.shape, f32),
            pltpu.VMEM(feat.shape, bf16),
            pltpu.VMEM(weight.shape, bf16),
            pltpu.VMEM(cot.shape, bf16),
            pltpu.SemaphoreType.DMA((8 + planes,)),
            pltpu.VMEM((tiles, 2 * YZ, TILE), bf16),
            pltpu.VMEM((tiles, 3 * GX, TILE), f32),
            pltpu.VMEM((tiles, 8, TILE), f32),
            pltpu.VMEM((16, pixels), bf16),
            pltpu.VMEM((IMG_ROW, ROWS, YZ), f32),
            pltpu.VMEM((2, ROWS, YZ), f32),
            pltpu.VMEM((2, ROWS, YZ), f32),
            pltpu.VMEM((IMG_ROW, USED, YZ), f32),
            pltpu.VMEM((IMG_ROW, 2 * USED, 2 * YZ), bf16),
            pltpu.VMEM((planes, OWN_MOST * COEF, YZ), f32),
            pltpu.VMEM((2, 128), f32),
            pltpu.VMEM((8, TILE), f32),
            pltpu.SMEM((images,), i32),
            pltpu.SMEM((images,), i32),
            pltpu.SMEM((images,), i32),
            pltpu.SMEM((planes * OWN_MOST,), i32),
            pltpu.VMEM((planes, OWN_MOST * 9, YZ), f32),
            pltpu.VMEM((planes, OWN_MOST * 9, YZ), f32),
            pltpu.VMEM((rows_x, IMG_ROW * 9, YZ), f32),
            pltpu.VMEM((groups, IMG_ROW * 9, YZ), f32),
            pltpu.VMEM((IMG_ROW * 9, YZ), f32),
            pltpu.VMEM((planes, IMG_ROW * 9, YZ), f32),
            pltpu.VMEM((planes, 2 * COEF, YZ), f32),
            pltpu.VMEM((planes, 2 * COEF, YZ), f32),
            pltpu.VMEM((2 * COEF, YZ), f32),
            pltpu.VMEM((groups + 1, 2 * COEF, YZ), f32),
            pltpu.VMEM((planes, OWN_MOST * COEF, YZ), f32),
            pltpu.VMEM((planes, OWN_MOST * COEF, YZ), f32),
            pltpu.VMEM((planes * groups, 2, 128), f32),
            pltpu.SemaphoreType.DMA((2,)),
            pltpu.SemaphoreType.DMA((2,)),
            pltpu.SemaphoreType.DMA((4, planes)),
            pltpu.SemaphoreType.DMA((4, planes)),
            pltpu.SemaphoreType.DMA((2, groups)),
            pltpu.SemaphoreType.DMA((2, groups)),
        ],
        compiler_params=pltpu.CompilerParams(
            collective_id=0, has_side_effects=True, vmem_limit_bytes=VMEM_LIMIT
        ),
    )(
        *(
            pltpu.with_memory_space_constraint(operand, pltpu.HBM)
            for operand in (
                ids,
                tile_image,
                bias,
                table_rows,
                cell_rows,
                frac,
                feat,
                weight,
                cot,
            )
        )
    )
    owned, head, bias_grad, fgrad = pl.pallas_call(
        finish,
        out_shape=(
            jax.ShapeDtypeStruct((COEF, OWN_MOST, CELLS), f32),
            jax.ShapeDtypeStruct(weight.shape, f32),
            jax.ShapeDtypeStruct(bias.shape, f32),
            jax.ShapeDtypeStruct(feat.shape, bf16),
        ),
        in_specs=[vmem, vmem, vmem],
        out_specs=(hbm, hbm, hbm, hbm),
        scratch_shapes=[
            pltpu.VMEM(weight.shape, f32),
            pltpu.VMEM(bias.shape, f32),
            pltpu.SemaphoreType.DMA((7,)),
        ],
        compiler_params=pltpu.CompilerParams(vmem_limit_bytes=16 << 20),
    )(owned, stat, fgrad)
    return jnp.transpose(owned, (1, 0, 2)), head, bias_grad, fgrad


def solution(mesh):
    rows_x = mesh.shape["img"]
    side = math.isqrt(mesh.shape["pix"] // 2)
    return jax.shard_map(
        functools.partial(shards, side, rows_x),
        mesh=mesh,
        in_specs=(
            P(),
            P(("img", "pix"), None, None),
            P(("img", "pix")),
            P(("img", "pix")),
            P(None, ("img", "pix")),
            P(None, ("img", "pix")),
            P(),
            P(),
            P(None, ("img", "pix")),
        ),
        out_specs=(P(("img", "pix"), None, None), P(), P(), P(None, ("img", "pix"))),
        check_vma=False,
    )
```

time: 44.6 us -> 37.4 us (0.84)
  Pallas kernels: 43.8 us -> 36.6 us
    pallas_call x1, Pallas kernels: 41.9 us -> 35.2 us  [shards(): pl.pallas_call(functools.partial(kernel, side, rows_x), out_shape=(jax.Sh...]
    pallas_call x1, Pallas kernels: 1.96 us -> 1.43 us  [shards(): pl.pallas_call(finish, out_shape=(jax.ShapeDtypeStruct((COEF, OWN_MOST, C...]
where the time goes in v3:
time: 37.4 us; the launch traced here: 37.3 us
  Pallas kernels  36.6 us (98%)
  between operations  0.64 us (2%)
    pallas_call x1, Pallas kernels, shards(): pl.pallas_call(functools.partial(kernel, side, rows_x), out_shape=(jax.Sh...  35.2 us
    pallas_call x1, Pallas kernels, shards(): pl.pallas_call(finish, out_shape=(jax.ShapeDtypeStruct((COEF, OWN_MOST, C...  1.43 us

profile of v3, /device:TPU:1, one launch (start us, length us, event | category | flops | bytes accessed | tf_op | source)
XLA Modules:
  0.0 37.3 jit_solution(16129948106007692178)
XLA Ops:
  0.6 35.2 %shard_map.120 = (f32[12,2,2048]{2,1,0:T(2,128)S(1)}, f32[2,128]{1,0:T(2,128)S(1)}, bf16[64,16384]{1,0:T(8,128)(2,1)S(1)}) custom-call(s32[16]{0:T(128)} %ids_any.1, s32[16]{0:T(128)} %tile_any.1, f32[3]{0:T(128)} %bias_any.1, f32[96,2048]{1,0:T(8,128)} %bitcast.5, s32[128,128]{1,0:T(8,128)} %bitcast.6, f32[3,16384]{1,0:T(4,128)} %frac_any.1, ...), custom_call_target="tpu_custom_call" | custom-call | tf_op jit(solution)/shard_map/pallas_call | solution.py:565
  35.8 1.4 %shard_map.121 = (f32[12,2,2048]{2,1,0:T(2,128)}, f32[3,64]{1,0:T(4,128)}, f32[3]{0:T(128)}, bf16[64,16384]{1,0:T(8,128)(2,1)}) custom-call(f32[12,2,2048]{2,1,0:T(2,128)S(1)} %get-tuple-element.11.owned_in, f32[2,128]{1,0:T(2,128)S(1)} %get-tuple-element.12.stat_in, bf16[64,16384]{1,0:T(8,128)(2,1)S(1)} %get-tuple-element.13.fgrad_in), custom_call_target="tpu_custom_call" | custom-call | tf_op jit(solution)/shard_map/pallas_call | solution.py:640

commit v4 on v3

--- a/solution.py
+++ b/solution.py
@@ -21,7 +21,6 @@
 USED = 9 * GX
 VMEM_LIMIT = 40 << 20
 SPLAT_UNROLL = 8
-SLICE_UNROLL = 16
 FEATURE_UNROLL = 8
 MESH = pl.DeviceIdType.MESH
 NT = (((1,), (1,)), ((), ()))
@@ -70,6 +69,7 @@
     uax_ref,
     colour_ref,
     half_ref,
+    feat_t_ref,
     acc_ref,
     sib_ref,
     total_ref,
@@ -77,7 +77,6 @@
     grid_ref,
     tv_ref,
     stat_ref,
-    bias_acc,
     holder_q,
     holder_g,
     rank_ref,
@@ -224,7 +223,6 @@
         fetch.start()
 
     acc_ref[...] = jnp.zeros_like(acc_ref)
-    bias_acc[...] = jnp.zeros_like(bias_acc)
     fetches[0].wait()
     holders = []
     ranks = []
@@ -344,7 +342,7 @@
             acc_ref[i] += jnp.where(image == i, grads, 0.0)
 
     def slice_tile(t):
-        px = pl.ds(pl.multiple_of(t * TILE, TILE), TILE)
+        px = slice(t * TILE, (t + 1) * TILE)
         wide = jnp.dot(
             grid_ref[tile_ref[t]], splat_ref[t], preferred_element_type=jnp.float32
         )
@@ -364,7 +362,7 @@
             jnp.bfloat16
         )
         half_ref[:, px] = d_half
-        bias_acc[...] += d_logits
+        return sum(d_logits[:, n : n + 128] for n in range(0, TILE, 128))
 
     def run(body, unroll):
         def step(n, carry):
@@ -409,6 +407,32 @@
         return carry
 
     lax.fori_loop(0, planes, find_dest, 0)
+
+    def turn_tile(t):
+        px = pl.ds(pl.multiple_of(t * TILE, TILE), TILE)
+        feat_t_ref[px, :] = feat_ref[:, px].T
+
+    def reduce_two():
+        plane_arrive(2, r1_recv)
+        total = r1_recv[0]
+        for q in range(1, planes):
+            total = total + r1_recv[q]
+        for i in range(2):
+            r2_send[i] = total[i * COEF : (i + 1) * COEF]
+        line_send(1, lambda g: r2_send, r2_recv)
+        r2_recv[my_g] = r2_send[...]
+        r2_recv[groups] = jnp.zeros_like(r2_send)
+
+    def reduce_three():
+        line_arrive(1, r2_recv)
+        for q in range(planes):
+            for s in range(OWN_MOST):
+                i = dest_ref[q * OWN_MOST + s]
+                r3_send[q, s] = r2_recv[i // 2, i % 2]
+        plane_send(3, lambda q: r3_send.at[q], r3_recv)
+        r3_recv[my_q] = r3_send[my_q]
+
+    reduce_two()
 
     lane = lax.broadcasted_iota(jnp.int32, (COEF, YZ), 1)
     for s in range(OWN_MOST):
@@ -430,35 +454,13 @@
                 before = jnp.where(first, here - pltpu.roll(here, step, 1), 0.0)
                 after = jnp.where(last, pltpu.roll(here, YZ - step, 1) - here, 0.0)
                 total = total + (before - after)
-            tv_ref[q, s * COEF : (s + 1) * COEF, :] = jnp.where(
-                own_has[s] == 1, total, 0.0
-            )
-
-    def reduce_two():
-        plane_arrive(2, r1_recv)
-        total = r1_recv[0]
-        for q in range(1, planes):
-            total = total + r1_recv[q]
-        r2_send[...] = total
-        line_send(1, lambda g: r2_send, r2_recv)
-        r2_recv[my_g] = total
-        r2_recv[groups] = jnp.zeros_like(total)
-
-    def reduce_three():
-        line_arrive(1, r2_recv)
-        for q in range(planes):
-            for s in range(OWN_MOST):
-                i = dest_ref[q * OWN_MOST + s]
-                r3_send[q, s * COEF : (s + 1) * COEF, :] = jnp.where(
-                    i % 2 == 0, r2_recv[i // 2, 0:COEF], r2_recv[i // 2, COEF:]
-                )
-        plane_send(3, lambda q: r3_send.at[q], r3_recv)
-        r3_recv[my_q] = r3_send[my_q]
-
-    reduce_two()
-    plane_arrive(1, g3_recv)
-    for i in range(IMG_ROW):
-        for q in range(planes):
+            tv_ref[q, s] = jnp.where(own_has[s] == 1, total, 0.0)
+
+    run(turn_tile, 8)
+    for q in [my_q] + plane_q[::-1]:
+        if q is not my_q:
+            plane_copy(1, q, g3_recv.at[q], g3_recv.at[q], q).wait_recv()
+        for i in range(IMG_ROW):
             grid_f32[i, pl.ds(q, 9, stride=GX), :] = g3_recv[q, i * 9 : (i + 1) * 9]
     for i in range(IMG_ROW):
         full = grid_f32[i]
@@ -469,12 +471,12 @@
         grid_ref[i, USED : 2 * USED, 0:YZ] = rest
         grid_ref[i, USED : 2 * USED, YZ : 2 * YZ] = rest
 
-    run(slice_tile, SLICE_UNROLL)
-
-    head = lax.dot_general(
-        half_ref[...], feat_ref[...], NT, preferred_element_type=jnp.float32
-    )
-    bias_sum = jnp.sum(bias_acc[...], axis=1, keepdims=True)
+    bias_part = sum(slice_tile(t) for t in range(tiles))
+
+    head = jnp.dot(
+        half_ref[...], feat_t_ref[...], preferred_element_type=jnp.float32
+    )
+    bias_sum = jnp.sum(bias_part, axis=1, keepdims=True)
     on_row = lax.broadcasted_iota(jnp.int32, (8, head.shape[1]), 0)
     on_lane = lax.broadcasted_iota(jnp.int32, (8, head.shape[1]), 1)
     bias_row = jnp.sum(
@@ -498,11 +500,7 @@
     plane_arrive(3, r3_recv)
     for q in range(planes):
         for s in range(OWN_MOST):
-            rows = slice(s * COEF, (s + 1) * COEF)
-            owned_ref[:, s, q * YZ : (q + 1) * YZ] = r3_recv[q, rows] + tv_ref[q, rows]
-    pltpu.make_async_copy(h1_recv, h1_recv, head_sems.at[1]).wait()
-    head_ref[...] = jnp.sum(h1_recv[...], axis=0)
-
+            owned_ref[:, s, q * YZ : (q + 1) * YZ] = r3_recv[q, s] + tv_ref[q, s]
     for q in plane_q:
         plane_copy(0, q, g1_send.at[q], g1_recv.at[my_q]).wait_send()
         plane_copy(1, q, g3_send, g3_recv.at[my_q]).wait_send()
@@ -511,6 +509,15 @@
     for g in line_g:
         line_copy(0, g, g2_send.at[g // 2], g2_recv.at[my_g]).wait_send()
         line_copy(1, g, r2_send, r2_recv.at[my_g]).wait_send()
+
+    pltpu.make_async_copy(h1_recv, h1_recv, head_sems.at[1]).wait()
+    count = h1_recv.shape[0]
+    sums = [
+        jnp.sum(h1_recv[n : n + count // 8], axis=0) for n in range(0, count, count // 8)
+    ]
+    while len(sums) > 1:
+        sums = [a + b for a, b in zip(sums[::2], sums[1::2])]
+    head_ref[...] = sums[0]
     sent = h1_recv.at[pl.ds(0, len(head_devs))]
     pltpu.make_async_copy(sent, sent, head_sems.at[0]).wait()
 
@@ -558,6 +565,7 @@
     groups = rows_x * 2
     images = ids.shape[0]
     f32, bf16, i32 = jnp.float32, jnp.bfloat16, jnp.int32
+    chunk = (COEF, YZ)
     vmem = pl.BlockSpec(memory_space=pltpu.VMEM)
     hbm = pl.BlockSpec(memory_space=pltpu.HBM)
     table_rows = jnp.transpose(table, (1, 0, 2)).reshape(-1, CELLS)
@@ -586,14 +594,14 @@
             pltpu.VMEM((tiles, 3 * GX, TILE), f32),
             pltpu.VMEM((tiles, 8, TILE), f32),
             pltpu.VMEM((16, pixels), bf16),
+            pltpu.VMEM((pixels, feat.shape[0]), bf16),
             pltpu.VMEM((IMG_ROW, ROWS, YZ), f32),
             pltpu.VMEM((2, ROWS, YZ), f32),
             pltpu.VMEM((2, ROWS, YZ), f32),
             pltpu.VMEM((IMG_ROW, USED, YZ), f32),
             pltpu.VMEM((IMG_ROW, 2 * USED, 2 * YZ), bf16),
-            pltpu.VMEM((planes, OWN_MOST * COEF, YZ), f32),
+            pltpu.VMEM((planes, OWN_MOST) + chunk, f32),
             pltpu.VMEM((2, 128), f32),
-            pltpu.VMEM((8, TILE), f32),
             pltpu.SMEM((images,), i32),
             pltpu.SMEM((images,), i32),
             pltpu.SMEM((images,), i32),
@@ -606,10 +614,10 @@
             pltpu.VMEM((planes, IMG_ROW * 9, YZ), f32),
             pltpu.VMEM((planes, 2 * COEF, YZ), f32),
             pltpu.VMEM((planes, 2 * COEF, YZ), f32),
-            pltpu.VMEM((2 * COEF, YZ), f32),
-            pltpu.VMEM((groups + 1, 2 * COEF, YZ), f32),
-            pltpu.VMEM((planes, OWN_MOST * COEF, YZ), f32),
-            pltpu.VMEM((planes, OWN_MOST * COEF, YZ), f32),
+            pltpu.VMEM((2,) + chunk, f32),
+            pltpu.VMEM((groups + 1, 2) + chunk, f32),
+            pltpu.VMEM((planes, OWN_MOST) + chunk, f32),
+            pltpu.VMEM((planes, OWN_MOST) + chunk, f32),
             pltpu.VMEM((planes * groups, 2, 128), f32),
             pltpu.SemaphoreType.DMA((2,)),
             pltpu.SemaphoreType.DMA((2,)),

time: 37.4 us -> 37 us (0.989)
  Pallas kernels: 36.6 us -> 36.2 us
    pallas_call x1, Pallas kernels: 35.2 us -> 34.8 us  [shards(): pl.pallas_call(functools.partial(kernel, side, rows_x), out_shape=(jax.Sh...]
where the time goes in v4:
time: 37 us; the launch traced here: 36.8 us
  Pallas kernels  36.2 us (98%)
  between operations  0.64 us (2%)
    pallas_call x1, Pallas kernels, shards(): pl.pallas_call(functools.partial(kernel, side, rows_x), out_shape=(jax.Sh...  34.8 us
    pallas_call x1, Pallas kernels, shards(): pl.pallas_call(finish, out_shape=(jax.ShapeDtypeStruct((COEF, OWN_MOST, C...  1.43 us

profile of v4, /device:TPU:1, one launch (start us, length us, event | category | flops | bytes accessed | tf_op | source)
XLA Modules:
  0.0 36.8 jit_solution(1705828472616995547)
XLA Ops:
  0.6 34.8 %shard_map.120 = (f32[12,2,2048]{2,1,0:T(2,128)S(1)}, f32[2,128]{1,0:T(2,128)S(1)}, bf16[64,16384]{1,0:T(8,128)(2,1)S(1)}) custom-call(s32[16]{0:T(128)} %ids_any.1, s32[16]{0:T(128)} %tile_any.1, f32[3]{0:T(128)} %bias_any.1, f32[96,2048]{1,0:T(8,128)} %bitcast.5, s32[128,128]{1,0:T(8,128)} %bitcast.6, f32[3,16384]{1,0:T(4,128)} %frac_any.1, ...), custom_call_target="tpu_custom_call" | custom-call | tf_op jit(solution)/shard_map/pallas_call | solution.py:573
  35.4 1.4 %shard_map.121 = (f32[12,2,2048]{2,1,0:T(2,128)}, f32[3,64]{1,0:T(4,128)}, f32[3]{0:T(128)}, bf16[64,16384]{1,0:T(8,128)(2,1)}) custom-call(f32[12,2,2048]{2,1,0:T(2,128)S(1)} %get-tuple-element.11.owned_in, f32[2,128]{1,0:T(2,128)S(1)} %get-tuple-element.12.stat_in, bf16[64,16384]{1,0:T(8,128)(2,1)S(1)} %get-tuple-element.13.fgrad_in), custom_call_target="tpu_custom_call" | custom-call | tf_op jit(solution)/shard_map/pallas_call | solution.py:648

commit v5 on v4

--- a/solution.py
+++ b/solution.py
@@ -20,7 +20,7 @@
 ROWS = COEF * GX
 USED = 9 * GX
 VMEM_LIMIT = 40 << 20
-SPLAT_UNROLL = 8
+SPLAT_UNROLL = 16
 FEATURE_UNROLL = 8
 MESH = pl.DeviceIdType.MESH
 NT = (((1,), (1,)), ((), ()))
@@ -119,7 +119,7 @@
     table_fetches = [
         pltpu.make_async_copy(
             table_any.at[:, pl.ds(q * YZ, YZ)],
-            table_ref.at[q],
+            table_ref.at[q, pl.ds(0, table_any.shape[0])],
             in_sems.at[len(operands) + q],
         )
         for q in range(planes)
@@ -127,7 +127,7 @@
     groups = rows_x * 2
     tiles = cell_ref.shape[0] // 8
     images = ids_ref.shape[0]
-    held = table_ref.shape[1] // COEF
+    held = table_any.shape[0] // COEF
     my_x = lax.axis_index("img")
     my_pix = lax.axis_index("pix")
     my_q = my_pix // 2
@@ -288,11 +288,11 @@
         line_arrive(0, g2_recv)
         for i in range(IMG_ROW):
             at = i * 9
-            g3_send[at : at + 9, :] = g2_recv[
+            g3_send[0, at : at + 9, :] = g2_recv[
                 holder_g[my_x * IMG_ROW + i], at : at + 9
             ]
-        plane_send(1, lambda q: g3_send, g3_recv)
-        g3_recv[my_q] = g3_send[...]
+        plane_send(1, lambda q: g3_send.at[0], g3_recv)
+        g3_recv[my_q] = g3_send[0]
 
     def splat_tile(t):
         px = pl.ds(pl.multiple_of(t * TILE, TILE), TILE)
@@ -386,7 +386,7 @@
     gather_two()
     sibling.wait()
     for i in range(2):
-        total_ref[i] = acc_ref[2 * my_c + i] + sib_ref[i]
+        total_ref[i, 0:ROWS] = acc_ref[2 * my_c + i] + sib_ref[i]
     for q in range(planes):
         for i in range(2):
             r1_send[q, i * COEF : (i + 1) * COEF, :] = total_ref[
@@ -463,7 +463,7 @@
         for i in range(IMG_ROW):
             grid_f32[i, pl.ds(q, 9, stride=GX), :] = g3_recv[q, i * 9 : (i + 1) * 9]
     for i in range(IMG_ROW):
-        full = grid_f32[i]
+        full = grid_f32[i, 0:USED]
         big = full.astype(jnp.bfloat16)
         rest = (full - big.astype(jnp.float32)).astype(jnp.bfloat16)
         grid_ref[i, 0:USED, 0:YZ] = big
@@ -503,7 +503,7 @@
             owned_ref[:, s, q * YZ : (q + 1) * YZ] = r3_recv[q, s] + tv_ref[q, s]
     for q in plane_q:
         plane_copy(0, q, g1_send.at[q], g1_recv.at[my_q]).wait_send()
-        plane_copy(1, q, g3_send, g3_recv.at[my_q]).wait_send()
+        plane_copy(1, q, g3_send.at[0], g3_recv.at[my_q]).wait_send()
         plane_copy(2, q, r1_send.at[q], r1_recv.at[my_q]).wait_send()
         plane_copy(3, q, r3_send.at[q], r3_recv.at[my_q]).wait_send()
     for g in line_g:
@@ -583,7 +583,7 @@
             pltpu.SMEM(ids.shape, i32),
             pltpu.SMEM(tile_image.shape, i32),
             pltpu.SMEM(bias.shape, f32),
-            pltpu.VMEM((planes, table_rows.shape[0], YZ), f32),
+            pltpu.VMEM((planes, table_rows.shape[0] * 16 // COEF, YZ), f32),
             pltpu.VMEM(cell_rows.shape, i32),
             pltpu.VMEM(frac.shape, f32),
             pltpu.VMEM(feat.shape, bf16),
@@ -597,8 +597,8 @@
             pltpu.VMEM((pixels, feat.shape[0]), bf16),
             pltpu.VMEM((IMG_ROW, ROWS, YZ), f32),
             pltpu.VMEM((2, ROWS, YZ), f32),
-            pltpu.VMEM((2, ROWS, YZ), f32),
-            pltpu.VMEM((IMG_ROW, USED, YZ), f32),
+            pltpu.VMEM((2, 16 * GX, YZ), f32),
+            pltpu.VMEM((IMG_ROW, 16 * GX, YZ), f32),
             pltpu.VMEM((IMG_ROW, 2 * USED, 2 * YZ), bf16),
             pltpu.VMEM((planes, OWN_MOST) + chunk, f32),
             pltpu.VMEM((2, 128), f32),
@@ -606,14 +606,14 @@
             pltpu.SMEM((images,), i32),
             pltpu.SMEM((images,), i32),
             pltpu.SMEM((planes * OWN_MOST,), i32),
-            pltpu.VMEM((planes, OWN_MOST * 9, YZ), f32),
-            pltpu.VMEM((planes, OWN_MOST * 9, YZ), f32),
-            pltpu.VMEM((rows_x, IMG_ROW * 9, YZ), f32),
-            pltpu.VMEM((groups, IMG_ROW * 9, YZ), f32),
-            pltpu.VMEM((IMG_ROW * 9, YZ), f32),
-            pltpu.VMEM((planes, IMG_ROW * 9, YZ), f32),
-            pltpu.VMEM((planes, 2 * COEF, YZ), f32),
-            pltpu.VMEM((planes, 2 * COEF, YZ), f32),
+            pltpu.VMEM((planes + 1, OWN_MOST * 9, YZ), f32),
+            pltpu.VMEM((planes + 1, OWN_MOST * 9, YZ), f32),
+            pltpu.VMEM((rows_x + 1, IMG_ROW * 9, YZ), f32),
+            pltpu.VMEM((groups + 1, IMG_ROW * 9, YZ), f32),
+            pltpu.VMEM((2, IMG_ROW * 9, YZ), f32),
+            pltpu.VMEM((planes + 1, IMG_ROW * 9, YZ), f32),
+            pltpu.VMEM((planes + 1, 2 * COEF, YZ), f32),
+            pltpu.VMEM((planes + 1, 2 * COEF, YZ), f32),
             pltpu.VMEM((2,) + chunk, f32),
             pltpu.VMEM((groups + 1, 2) + chunk, f32),
             pltpu.VMEM((planes, OWN_MOST) + chunk, f32),

time: 37 us -> 36.8 us (level)
  no operation moved by 1% of the time
where the time goes in v5:
time: 36.8 us; the launch traced here: 36.7 us
  Pallas kernels  36.1 us (98%)
  between operations  0.64 us (2%)
    pallas_call x1, Pallas kernels, shards(): pl.pallas_call(functools.partial(kernel, side, rows_x), out_shape=(jax.Sh...  34.6 us
    pallas_call x1, Pallas kernels, shards(): pl.pallas_call(finish, out_shape=(jax.ShapeDtypeStruct((COEF, OWN_MOST, C...  1.43 us

profile of v5, /device:TPU:1, one launch (start us, length us, event | category | flops | bytes accessed | tf_op | source)
XLA Modules:
  0.0 36.7 jit_solution(15361144156432894592)
XLA Ops:
  0.6 34.6 %shard_map.120 = (f32[12,2,2048]{2,1,0:T(2,128)S(1)}, f32[2,128]{1,0:T(2,128)S(1)}, bf16[64,16384]{1,0:T(8,128)(2,1)S(1)}) custom-call(s32[16]{0:T(128)} %ids_any.1, s32[16]{0:T(128)} %tile_any.1, f32[3]{0:T(128)} %bias_any.1, f32[96,2048]{1,0:T(8,128)} %bitcast.5, s32[128,128]{1,0:T(8,128)} %bitcast.6, f32[3,16384]{1,0:T(4,128)} %frac_any.1, ...), custom_call_target="tpu_custom_call" | custom-call | tf_op jit(solution)/shard_map/pallas_call | solution.py:573
  35.3 1.4 %shard_map.121 = (f32[12,2,2048]{2,1,0:T(2,128)}, f32[3,64]{1,0:T(4,128)}, f32[3]{0:T(128)}, bf16[64,16384]{1,0:T(8,128)(2,1)}) custom-call(f32[12,2,2048]{2,1,0:T(2,128)S(1)} %get-tuple-element.11.owned_in, f32[2,128]{1,0:T(2,128)S(1)} %get-tuple-element.12.stat_in, bf16[64,16384]{1,0:T(8,128)(2,1)S(1)} %get-tuple-element.13.fgrad_in), custom_call_target="tpu_custom_call" | custom-call | tf_op jit(solution)/shard_map/pallas_call | solution.py:648

commit v6 on v5

--- a/solution.py
+++ b/solution.py
@@ -397,17 +397,6 @@
 
     gather_three()
 
-    def find_dest(q, carry):
-        dev = my_x * (planes * 2) + q * 2 + my_c
-        for s in range(OWN_MOST):
-            found = jnp.int32(images)
-            for i in range(images):
-                found = jnp.where((holders[i] == dev) & (ranks[i] == s), i, found)
-            dest_ref[q * OWN_MOST + s] = found
-        return carry
-
-    lax.fori_loop(0, planes, find_dest, 0)
-
     def turn_tile(t):
         px = pl.ds(pl.multiple_of(t * TILE, TILE), TILE)
         feat_t_ref[px, :] = feat_ref[:, px].T
@@ -433,6 +422,18 @@
         r3_recv[my_q] = r3_send[my_q]
 
     reduce_two()
+
+    def find_dest(q, carry):
+        dev = my_x * (planes * 2) + q * 2 + my_c
+        for s in range(OWN_MOST):
+            found = jnp.int32(images)
+            for i in range(images):
+                found = jnp.where((holders[i] == dev) & (ranks[i] == s), i, found)
+            dest_ref[q * OWN_MOST + s] = found
+        return carry
+
+    lax.fori_loop(0, planes, find_dest, 0)
+
 
     lane = lax.broadcasted_iota(jnp.int32, (COEF, YZ), 1)
     for s in range(OWN_MOST):

time: 36.8 us -> 36.8 us (level)
  no operation moved by 1% of the time
where the time goes in v6:
time: 36.8 us; the launch traced here: 36.7 us
  Pallas kernels  36.1 us (98%)
  between operations  0.64 us (2%)
    pallas_call x1, Pallas kernels, shards(): pl.pallas_call(functools.partial(kernel, side, rows_x), out_shape=(jax.Sh...  34.6 us
    pallas_call x1, Pallas kernels, shards(): pl.pallas_call(finish, out_shape=(jax.ShapeDtypeStruct((COEF, OWN_MOST, C...  1.43 us

profile of v6, /device:TPU:1, one launch (start us, length us, event | category | flops | bytes accessed | tf_op | source)
XLA Modules:
  0.0 36.7 jit_solution(4627617126832190588)
XLA Ops:
  0.6 34.6 %shard_map.120 = (f32[12,2,2048]{2,1,0:T(2,128)S(1)}, f32[2,128]{1,0:T(2,128)S(1)}, bf16[64,16384]{1,0:T(8,128)(2,1)S(1)}) custom-call(s32[16]{0:T(128)} %ids_any.1, s32[16]{0:T(128)} %tile_any.1, f32[3]{0:T(128)} %bias_any.1, f32[96,2048]{1,0:T(8,128)} %bitcast.5, s32[128,128]{1,0:T(8,128)} %bitcast.6, f32[3,16384]{1,0:T(4,128)} %frac_any.1, ...), custom_call_target="tpu_custom_call" | custom-call | tf_op jit(solution)/shard_map/pallas_call | solution.py:574
  35.3 1.4 %shard_map.121 = (f32[12,2,2048]{2,1,0:T(2,128)}, f32[3,64]{1,0:T(4,128)}, f32[3]{0:T(128)}, bf16[64,16384]{1,0:T(8,128)(2,1)}) custom-call(f32[12,2,2048]{2,1,0:T(2,128)S(1)} %get-tuple-element.11.owned_in, f32[2,128]{1,0:T(2,128)S(1)} %get-tuple-element.12.stat_in, bf16[64,16384]{1,0:T(8,128)(2,1)S(1)} %get-tuple-element.13.fgrad_in), custom_call_target="tpu_custom_call" | custom-call | tf_op jit(solution)/shard_map/pallas_call | solution.py:649

commit v7 on v5

--- a/solution.py
+++ b/solution.py
@@ -21,7 +21,7 @@
 USED = 9 * GX
 VMEM_LIMIT = 40 << 20
 SPLAT_UNROLL = 16
-FEATURE_UNROLL = 8
+FEATURE_UNROLL = 16
 MESH = pl.DeviceIdType.MESH
 NT = (((1,), (1,)), ((), ()))
 

time: 36.8 us -> 36.8 us (level)
  no operation moved by 1% of the time
where the time goes in v7:
time: 36.8 us; the launch traced here: 36.7 us
  Pallas kernels  36.1 us (98%)
  between operations  0.64 us (2%)
    pallas_call x1, Pallas kernels, shards(): pl.pallas_call(functools.partial(kernel, side, rows_x), out_shape=(jax.Sh...  34.6 us
    pallas_call x1, Pallas kernels, shards(): pl.pallas_call(finish, out_shape=(jax.ShapeDtypeStruct((COEF, OWN_MOST, C...  1.43 us

profile of v7, /device:TPU:1, one launch (start us, length us, event | category | flops | bytes accessed | tf_op | source)
XLA Modules:
  0.0 36.7 jit_solution(17291231436946076150)
XLA Ops:
  0.6 34.6 %shard_map.120 = (f32[12,2,2048]{2,1,0:T(2,128)S(1)}, f32[2,128]{1,0:T(2,128)S(1)}, bf16[64,16384]{1,0:T(8,128)(2,1)S(1)}) custom-call(s32[16]{0:T(128)} %ids_any.1, s32[16]{0:T(128)} %tile_any.1, f32[3]{0:T(128)} %bias_any.1, f32[96,2048]{1,0:T(8,128)} %bitcast.5, s32[128,128]{1,0:T(8,128)} %bitcast.6, f32[3,16384]{1,0:T(4,128)} %frac_any.1, ...), custom_call_target="tpu_custom_call" | custom-call | tf_op jit(solution)/shard_map/pallas_call | solution.py:573
  35.3 1.4 %shard_map.121 = (f32[12,2,2048]{2,1,0:T(2,128)}, f32[3,64]{1,0:T(4,128)}, f32[3]{0:T(128)}, bf16[64,16384]{1,0:T(8,128)(2,1)}) custom-call(f32[12,2,2048]{2,1,0:T(2,128)S(1)} %get-tuple-element.11.owned_in, f32[2,128]{1,0:T(2,128)S(1)} %get-tuple-element.12.stat_in, bf16[64,16384]{1,0:T(8,128)(2,1)S(1)} %get-tuple-element.13.fgrad_in), custom_call_target="tpu_custom_call" | custom-call | tf_op jit(solution)/shard_map/pallas_call | solution.py:648
